TPU v7x, 32 devices: a whole 2x2x4 slice. The times are simulated.
32 devices in a mesh: fsdp: 4 (over y, core), ctx: 4 (over z), tensor: 2 (over x).
Axes of the slice: x: 2, y: 2, z: 4, core: 2. Of those that a mesh axis runs over, the one named last changes fastest.
Arguments:
- tokens: bfloat16 [8, 1024, 2048], P('fsdp', 'ctx'), may hold values from -6 to 6
- segments: int32 [8, 1024], P('fsdp'), may hold values from 0 to 24, as said below
- cotangent: bfloat16 [8, 1024, 2048], P('fsdp', 'ctx'), may hold values from -6 to 6
- attn_gain: bfloat16 [2048], P(('fsdp', 'ctx')), may hold values from 0.5 to 1.5
- w_query: bfloat16 [2048, 2048], P(('fsdp', 'ctx'), 'tensor'), may hold values from -0.1875 to 0.1875
- w_key: bfloat16 [2048, 2048], P(('fsdp', 'ctx'), 'tensor'), may hold values from -0.1875 to 0.1875
- w_value: bfloat16 [2048, 2048], P(('fsdp', 'ctx'), 'tensor'), may hold values from -0.125 to 0.125
- w_out: bfloat16 [2048, 2048], P('tensor', ('fsdp', 'ctx')), may hold values from -0.5 to 0.5
- mlp_gain: bfloat16 [2048], P(('fsdp', 'ctx')), may hold values from 0.5 to 1.5
- w_gate: bfloat16 [2048, 8192], P(('fsdp', 'ctx'), 'tensor'), may hold values from -0.125 to 0.125
- w_up: bfloat16 [2048, 8192], P(('fsdp', 'ctx'), 'tensor'), may hold values from -0.125 to 0.125
- w_down: bfloat16 [8192, 2048], P('tensor', ('fsdp', 'ctx')), may hold values from -0.125 to 0.125
Outputs:
- block_out: bfloat16 [8, 1024, 2048], P('fsdp', 'ctx')
- grad_tokens: float32 [8, 1024, 2048], P('fsdp', 'ctx')
- grad_attn_gain: float32 [2048], P(('fsdp', 'ctx'))
- grad_query: float32 [2048, 2048], P(('fsdp', 'ctx'), 'tensor')
- grad_key: float32 [2048, 2048], P(('fsdp', 'ctx'), 'tensor')
- grad_value: float32 [2048, 2048], P(('fsdp', 'ctx'), 'tensor')
- grad_out: float32 [2048, 2048], P('tensor', ('fsdp', 'ctx'))
- grad_mlp_gain: float32 [2048], P(('fsdp', 'ctx'))
- grad_gate: float32 [2048, 8192], P(('fsdp', 'ctx'), 'tensor')
- grad_up: float32 [2048, 8192], P(('fsdp', 'ctx'), 'tensor')
- grad_down: float32 [8192, 2048], P('tensor', ('fsdp', 'ctx'))
Inputs may be any that keep to these rules, and one draw needn't show every extreme that they name: `segments`: segment numbers start at 0 in every sequence and never fall; a document has 42 to 512 tokens except the last of a sequence, which may be shorter; of the 2 sequences that share one index of fsdp, one (drawn) is a single document; in one drawn index of fsdp, another of its sequences is cut into documents of exactly 42 tokens (the last may be shorter).
All inputs are finite; a program needn't handle non-finite values.
Results may differ from a plain program's by a relative error of at most 0.017.
Values may be sent and summed in bfloat16 or wider, within the bound.
No kernel may reach another device: no remote copies, remote signals or barrier semaphores. Data moves between devices by JAX's collectives and lax.ppermute only.
A program may use at most 384 MiB of HBM per device.

v0:
```python
import jax
import jax.numpy as jnp
from jax import lax
from jax.sharding import PartitionSpec as P

HEAD_DIM = 64


NORM_EPS = 1e-05
ROPE_BASE = 130000.0
MASKED = -1e30


def rms_scale(values, gain):
    return values * lax.rsqrt(jnp.mean(values * values, axis=-1, keepdims=True) + NORM_EPS) * gain


def doc_positions(segment_ids):
    places = jnp.arange(segment_ids.shape[0], dtype=jnp.int32)
    before = jnp.concatenate([segment_ids[:1] - 1, segment_ids[:-1]])
    starts = jnp.where(segment_ids != before, places, jnp.zeros_like(places))
    return places - lax.cummax(starts, axis=0)


def rope_tables(positions, head_dim):
    half_dim = head_dim // 2
    frequency = ROPE_BASE ** (-jnp.arange(half_dim, dtype=jnp.float32) * 2.0 / head_dim)
    angles = positions.astype(jnp.float32)[:, None] * frequency[None, :]
    return (jnp.cos(angles)[:, None, :], jnp.sin(angles)[:, None, :])


def rotate(values, cosine, sine_part):
    half_dim = values.shape[-1] // 2
    first_half = values[..., :half_dim]
    second_half = values[..., half_dim:]
    return jnp.concatenate(
        [
            first_half * cosine - second_half * sine_part,
            second_half * cosine + first_half * sine_part,
        ],
        axis=-1,
    )


def fetch_attention(attn_gain, w_query, w_key, w_value, w_out):
    return (
        lax.all_gather(attn_gain, ("fsdp", "ctx"), axis=0, tiled=True),
        lax.all_gather(w_query, ("fsdp", "ctx"), axis=0, tiled=True),
        lax.all_gather(w_key, ("fsdp", "ctx"), axis=0, tiled=True),
        lax.all_gather(w_value, ("fsdp", "ctx"), axis=0, tiled=True),
        lax.all_gather(w_out, ("fsdp", "ctx"), axis=1, tiled=True),
    )


def fetch_feedforward(mlp_gain, w_gate, w_up, w_down):
    return (
        lax.all_gather(mlp_gain, ("fsdp", "ctx"), axis=0, tiled=True),
        lax.all_gather(w_gate, ("fsdp", "ctx"), axis=0, tiled=True),
        lax.all_gather(w_up, ("fsdp", "ctx"), axis=0, tiled=True),
        lax.all_gather(w_down, ("fsdp", "ctx"), axis=1, tiled=True),
    )


def settle_attention(parts):
    return (
        lax.psum_scatter(parts[0], ("fsdp", "ctx"), scatter_dimension=0, tiled=True),
        lax.psum_scatter(parts[1], ("fsdp", "ctx"), scatter_dimension=0, tiled=True),
        lax.psum_scatter(parts[2], ("fsdp", "ctx"), scatter_dimension=0, tiled=True),
        lax.psum_scatter(parts[3], ("fsdp", "ctx"), scatter_dimension=0, tiled=True),
        lax.psum_scatter(parts[4], ("fsdp", "ctx"), scatter_dimension=1, tiled=True),
    )


def settle_feedforward(parts):
    return (
        lax.psum_scatter(parts[0], ("fsdp", "ctx"), scatter_dimension=0, tiled=True),
        lax.psum_scatter(parts[1], ("fsdp", "ctx"), scatter_dimension=0, tiled=True),
        lax.psum_scatter(parts[2], ("fsdp", "ctx"), scatter_dimension=0, tiled=True),
        lax.psum_scatter(parts[3], ("fsdp", "ctx"), scatter_dimension=1, tiled=True),
    )


def masked_scores(queries, keys_all, allowed):
    scores = (
        jnp.einsum("qhd,khd->hqk", queries, keys_all, preferred_element_type=jnp.float32) * 0.125
    )
    return jnp.where(allowed[None], scores, MASKED)


def project(normed_low, weight, row_count):
    return jnp.dot(normed_low, weight, preferred_element_type=jnp.float32).reshape(
        row_count, -1, HEAD_DIM
    )


def per_device(
    tokens,
    segments,
    cotangent,
    attn_gain,
    w_query,
    w_key,
    w_value,
    w_out,
    mlp_gain,
    w_gate,
    w_up,
    w_down,
):
    row_count = tokens.shape[1]
    seq_len = segments.shape[1]
    heads_here = w_query.shape[1] // HEAD_DIM
    offset = lax.axis_index("ctx") * row_count
    query_places = offset + jnp.arange(row_count, dtype=jnp.int32)
    key_places = jnp.arange(seq_len, dtype=jnp.int32)
    attn_totals = None
    mlp_totals = None
    outputs = []
    input_grads = []
    for micro_batch in range(tokens.shape[0]):
        segment_ids = segments[micro_batch]
        positions = lax.dynamic_slice_in_dim(doc_positions(segment_ids), offset, row_count)
        local_ids = lax.dynamic_slice_in_dim(segment_ids, offset, row_count)
        allowed = (local_ids[:, None] == segment_ids[None, :]) & (
            key_places[None, :] <= query_places[:, None]
        )
        cosine, sine_part = rope_tables(positions, HEAD_DIM)
        inputs = tokens[micro_batch].astype(jnp.float32)
        attn_set = fetch_attention(attn_gain, w_query, w_key, w_value, w_out)
        gain_one, query_full, key_full, value_full, out_full = attn_set
        gain_one_f = gain_one.astype(jnp.float32)
        normed_low = rms_scale(inputs, gain_one_f).astype(jnp.bfloat16)
        queries = rotate(project(normed_low, query_full, row_count), cosine, sine_part).astype(
            jnp.bfloat16
        )
        keys_local = rotate(project(normed_low, key_full, row_count), cosine, sine_part).astype(
            jnp.bfloat16
        )
        values_local = project(normed_low, value_full, row_count).astype(jnp.bfloat16)
        keys_flat, values_flat = (
            lax.all_gather(keys_local.reshape(row_count, -1), "ctx", axis=0, tiled=True),
            lax.all_gather(values_local.reshape(row_count, -1), "ctx", axis=0, tiled=True),
        )
        keys_all = keys_flat.reshape(seq_len, heads_here, HEAD_DIM)
        values_all = values_flat.reshape(seq_len, heads_here, HEAD_DIM)
        scores = masked_scores(queries, keys_all, allowed)
        row_peak = jnp.max(scores, axis=-1, keepdims=True)
        log_total = row_peak + jnp.log(jnp.sum(jnp.exp(scores - row_peak), axis=-1, keepdims=True))
        attn_probs = jnp.exp(scores - log_total).astype(jnp.bfloat16)
        attended = jnp.einsum(
            "hqk,khd->qhd", attn_probs, values_all, preferred_element_type=jnp.float32
        )
        attended = attended.reshape(row_count, -1).astype(jnp.bfloat16)
        attn_sum = lax.psum(
            jnp.dot(attended, out_full, preferred_element_type=jnp.float32), "tensor"
        )
        residual = inputs + attn_sum
        mlp_set = fetch_feedforward(mlp_gain, w_gate, w_up, w_down)
        gain_two, gate_full, up_full, down_full = mlp_set
        gain_two_f = gain_two.astype(jnp.float32)
        normed_two_low = rms_scale(residual, gain_two_f).astype(jnp.bfloat16)
        gate_proj = jnp.dot(normed_two_low, gate_full, preferred_element_type=jnp.float32)
        up_proj = jnp.dot(normed_two_low, up_full, preferred_element_type=jnp.float32)
        hidden = (jax.nn.silu(gate_proj) * up_proj).astype(jnp.bfloat16)
        mlp_sum = lax.psum(
            jnp.dot(hidden, down_full, preferred_element_type=jnp.float32).astype(jnp.bfloat16),
            "tensor",
        ).astype(jnp.float32)
        outputs.append((residual + mlp_sum).astype(jnp.bfloat16))
        back_mlp = fetch_feedforward(mlp_gain, w_gate, w_up, w_down)
        gain_two, gate_full, up_full, down_full = back_mlp
        upstream_low = cotangent[micro_batch]
        upstream = upstream_low.astype(jnp.float32)
        down_grad = jnp.einsum(
            "tf,td->fd", hidden, upstream_low, preferred_element_type=jnp.float32
        )
        hidden_grad = jnp.einsum(
            "td,fd->tf", upstream_low, down_full, preferred_element_type=jnp.float32
        )
        _, swiglu_back = jax.vjp(
            lambda gate_in, up_in: jax.nn.silu(gate_in) * up_in, gate_proj, up_proj
        )
        gate_grad, up_grad = swiglu_back(hidden_grad)
        gate_grad = gate_grad.astype(jnp.bfloat16)
        up_grad = up_grad.astype(jnp.bfloat16)
        gate_weight_grad = jnp.einsum(
            "td,tf->df", normed_two_low, gate_grad, preferred_element_type=jnp.float32
        )
        up_weight_grad = jnp.einsum(
            "td,tf->df", normed_two_low, up_grad, preferred_element_type=jnp.float32
        )
        back_two = jnp.einsum("tf,df->td", gate_grad, gate_full, preferred_element_type=jnp.float32)
        back_two = back_two + jnp.einsum(
            "tf,df->td", up_grad, up_full, preferred_element_type=jnp.float32
        )
        back_two = lax.psum(back_two, "tensor")
        _, norm_two_back = jax.vjp(rms_scale, residual, gain_two.astype(jnp.float32))
        residual_grad, gain_two_grad = norm_two_back(back_two)
        residual_grad = residual_grad + upstream
        back_attn = fetch_attention(attn_gain, w_query, w_key, w_value, w_out)
        gain_one, query_full, key_full, value_full, out_full = back_attn
        residual_low = residual_grad.astype(jnp.bfloat16)
        out_weight_grad = jnp.einsum(
            "tc,td->cd", attended, residual_low, preferred_element_type=jnp.float32
        )
        attended_grad = jnp.einsum(
            "td,cd->tc", residual_low, out_full, preferred_element_type=jnp.float32
        )
        attended_grad = attended_grad.astype(jnp.bfloat16).reshape(row_count, heads_here, HEAD_DIM)
        scores = masked_scores(queries, keys_all, allowed)
        soft_full = jnp.exp(scores - log_total)
        soft_low = soft_full.astype(jnp.bfloat16)
        probs_grad = jnp.einsum(
            "qhd,khd->hqk", attended_grad, values_all, preferred_element_type=jnp.float32
        )
        inner_sum = jnp.sum(soft_full * probs_grad, axis=-1, keepdims=True)
        scores_grad = (soft_full * (probs_grad - inner_sum)).astype(jnp.bfloat16)
        query_grad = 0.125 * jnp.einsum(
            "hqk,khd->qhd", scores_grad, keys_all, preferred_element_type=jnp.float32
        )
        key_terms = 0.125 * jnp.einsum(
            "hqk,qhd->khd", scores_grad, queries, preferred_element_type=jnp.float32
        )
        value_terms = jnp.einsum(
            "hqk,qhd->khd", soft_low, attended_grad, preferred_element_type=jnp.float32
        )
        key_grads, value_grads = (
            lax.psum_scatter(
                key_terms.reshape(seq_len, -1).astype(jnp.bfloat16),
                "ctx",
                scatter_dimension=0,
                tiled=True,
            ).astype(jnp.float32),
            lax.psum_scatter(
                value_terms.reshape(seq_len, -1).astype(jnp.bfloat16),
                "ctx",
                scatter_dimension=0,
                tiled=True,
            ).astype(jnp.float32),
        )
        _, rope_back = jax.vjp(lambda head_in: rotate(head_in, cosine, sine_part), query_grad)
        query_raw = rope_back(query_grad)[0].reshape(row_count, -1).astype(jnp.bfloat16)
        key_raw = (
            rope_back(key_grads.reshape(row_count, heads_here, HEAD_DIM))[0]
            .reshape(row_count, -1)
            .astype(jnp.bfloat16)
        )
        value_raw = value_grads.astype(jnp.bfloat16)
        query_weight_grad = jnp.einsum(
            "td,tc->dc", normed_low, query_raw, preferred_element_type=jnp.float32
        )
        key_weight_grad = jnp.einsum(
            "td,tc->dc", normed_low, key_raw, preferred_element_type=jnp.float32
        )
        value_weight_grad = jnp.einsum(
            "td,tc->dc", normed_low, value_raw, preferred_element_type=jnp.float32
        )
        back_one = jnp.einsum(
            "tc,dc->td", query_raw, query_full, preferred_element_type=jnp.float32
        )
        back_one = back_one + jnp.einsum(
            "tc,dc->td", key_raw, key_full, preferred_element_type=jnp.float32
        )
        back_one = back_one + jnp.einsum(
            "tc,dc->td", value_raw, value_full, preferred_element_type=jnp.float32
        )
        back_one = lax.psum(back_one.astype(jnp.bfloat16), "tensor").astype(jnp.float32)
        _, norm_one_back = jax.vjp(rms_scale, inputs, gain_one.astype(jnp.float32))
        inputs_grad, gain_one_grad = norm_one_back(back_one)
        input_grads.append(inputs_grad + residual_grad)
        attn_parts = (
            gain_one_grad,
            query_weight_grad,
            key_weight_grad,
            value_weight_grad,
            out_weight_grad,
        )
        mlp_parts = (gain_two_grad, gate_weight_grad, up_weight_grad, down_grad)
        attn_totals = (
            attn_parts if attn_totals is None else jax.tree.map(jnp.add, attn_totals, attn_parts)
        )
        mlp_totals = (
            mlp_parts if mlp_totals is None else jax.tree.map(jnp.add, mlp_totals, mlp_parts)
        )
    attn_totals = settle_attention(attn_totals)
    mlp_totals = settle_feedforward(mlp_totals)
    block_out = jnp.stack(outputs)
    grad_tokens = jnp.stack(input_grads)
    return (
        block_out,
        grad_tokens,
        attn_totals[0],
        attn_totals[1],
        attn_totals[2],
        attn_totals[3],
        attn_totals[4],
        mlp_totals[0],
        mlp_totals[1],
        mlp_totals[2],
        mlp_totals[3],
    )


def solution(mesh):
    return jax.shard_map(
        per_device,
        mesh=mesh,
        in_specs=(
            P("fsdp", "ctx", None),
            P("fsdp", None),
            P("fsdp", "ctx", None),
            P(("fsdp", "ctx")),
            P(("fsdp", "ctx"), "tensor"),
            P(("fsdp", "ctx"), "tensor"),
            P(("fsdp", "ctx"), "tensor"),
            P("tensor", ("fsdp", "ctx")),
            P(("fsdp", "ctx")),
            P(("fsdp", "ctx"), "tensor"),
            P(("fsdp", "ctx"), "tensor"),
            P("tensor", ("fsdp", "ctx")),
        ),
        out_specs=(
            P("fsdp", "ctx", None),
            P("fsdp", "ctx", None),
            P(("fsdp", "ctx")),
            P(("fsdp", "ctx"), "tensor"),
            P(("fsdp", "ctx"), "tensor"),
            P(("fsdp", "ctx"), "tensor"),
            P("tensor", ("fsdp", "ctx")),
            P(("fsdp", "ctx")),
            P(("fsdp", "ctx"), "tensor"),
            P(("fsdp", "ctx"), "tensor"),
            P("tensor", ("fsdp", "ctx")),
        ),
        check_vma=False,
    )
```

profile of v0, /device:TPU:0, one launch (start us, length us, event | category | flops | bytes accessed | tf_op | source)
XLA Modules:
  0.0 2884.2 jit_solution(12727060990958989365)
XLA Ops:
  9.4 33.9 %all-gather = bf16[16,1,128]{2,1,0:T(2,128)(2,1)S(1)} all-gather(bf16[1,1,128]{2,1,0:T(2,128)(2,1)} %bitcast.339), channel_id=1, replica_groups=mesh['fsdp'=4,'ctx'=4,'tensor'=2] {'fsdp','ctx'}, dimensions={0}, use_global_device_ids=true | all-gather | bytes 4352 | tf_op jit(solution)/shard_map/all_gather | solution.py:47
  69.9 45.1 %all-gather.20.cloned.1.call-done = bf16[2048,1024]{1,0:T(8,128)(2,1)} async-done(((bf16[128,1024]{1,0:T(8,128)(2,1)}), bf16[2048,1024]{1,0:T(8,128)(2,1)}) %all-gather.20.cloned.1.call-update) | async-done | bytes 4194320 | tf_op jit(solution)/shard_map/all_gather | solution.py:49
  135.5 31.0 %all-gather.14.cloned.1.call-done = bf16[2048,1024]{1,0:T(8,128)(2,1)} async-done(((bf16[128,1024]{1,0:T(8,128)(2,1)}), bf16[2048,1024]{1,0:T(8,128)(2,1)}) %all-gather.14.cloned.1.call-update) | async-done | bytes 4194320 | tf_op jit(solution)/shard_map/all_gather | solution.py:50
  183.8 29.4 %all-gather.34.cloned.1.call-done = bf16[1024,1024]{0,1:T(8,128)(2,1)} async-done(((bf16[256,1024]{0,1:T(8,128)(2,1)}), bf16[1024,1024]{0,1:T(8,128)(2,1)}) %all-gather.34.cloned.1.call-update) | async-done | bytes 2097168 | tf_op jit(solution)/shard_map/all_gather | solution.py:141
  223.9 35.8 %all-gather.22.cloned.1.call-done = bf16[1024,1024]{0,1:T(8,128)(2,1)} async-done(((bf16[256,1024]{0,1:T(8,128)(2,1)}), bf16[1024,1024]{0,1:T(8,128)(2,1)}) %all-gather.22.cloned.1.call-update) | async-done | bytes 2097168 | tf_op jit(solution)/shard_map/all_gather | solution.py:141
  270.3 35.9 %all-gather.32.cloned.1.call-done = bf16[1024,1024]{0,1:T(8,128)(2,1)} async-done(((bf16[256,1024]{0,1:T(8,128)(2,1)}), bf16[1024,1024]{0,1:T(8,128)(2,1)}) %all-gather.32.cloned.1.call-update) | async-done | bytes 2097168 | tf_op jit(solution)/shard_map/all_gather | solution.py:142
  314.8 38.1 %all-gather.16.cloned.1.call-done = bf16[1024,1024]{0,1:T(8,128)(2,1)} async-done(((bf16[256,1024]{0,1:T(8,128)(2,1)}), bf16[1024,1024]{0,1:T(8,128)(2,1)}) %all-gather.16.cloned.1.call-update) | async-done | bytes 2097168 | tf_op jit(solution)/shard_map/all_gather | solution.py:142
  361.4 45.0 %all-gather.24.cloned.1.call-done = bf16[1024,2048]{1,0:T(8,128)(2,1)} async-done(((bf16[1024,128]{1,0:T(8,128)(2,1)}), bf16[1024,2048]{1,0:T(8,128)(2,1)}) %all-gather.24.cloned.1.call-update) | async-done | bytes 4194320 | tf_op jit(solution)/shard_map/all_gather | solution.py:51
  416.1 29.6 %all-gather.1 = bf16[16,1,128]{2,1,0:T(2,128)(2,1)S(1)} all-gather(bf16[1,1,128]{2,1,0:T(2,128)(2,1)S(1)} %bitcast.340), channel_id=1, replica_groups=mesh['fsdp'=4,'ctx'=4,'tensor'=2] {'fsdp','ctx'}, dimensions={0}, use_global_device_ids=true | all-gather | bytes 4352 | tf_op jit(solution)/shard_map/all_gather | solution.py:57
  445.7 74.8 %all-reduce.20.cloned.1.call-done = (f32[256,2048]{1,0:T(8,128)}, f32[256,2048]{1,0:T(8,128)}) async-done(((f32[256,2048]{1,0:T(8,128)}, f32[256,2048]{1,0:T(8,128)}), (f32[256,2048]{1,0:T(8,128)}, f32[256,2048]{1,0:T(8,128)})) %all-reduce.20.cloned.1.call-update) | async-done | bytes 4194320 | tf_op jit(solution)/shard_map/psum | solution.py:154
  525.8 124.0 %all-gather.26.cloned.1.call-done = bf16[2048,4096]{1,0:T(8,128)(2,1)} async-done(((bf16[128,4096]{1,0:T(8,128)(2,1)}), bf16[2048,4096]{1,0:T(8,128)(2,1)}) %all-gather.26.cloned.1.call-update) | async-done | bytes 16777232 | tf_op jit(solution)/shard_map/all_gather | solution.py:58
  659.9 117.4 %all-gather.28.cloned.1.call-done = bf16[2048,4096]{1,0:T(8,128)(2,1)} async-done(((bf16[128,4096]{1,0:T(8,128)(2,1)}), bf16[2048,4096]{1,0:T(8,128)(2,1)}) %all-gather.28.cloned.1.call-update) | async-done | bytes 16777232 | tf_op jit(solution)/shard_map/all_gather | solution.py:59
  806.6 101.3 %all-gather.30.cloned.1.call-done = bf16[4096,2048]{1,0:T(8,128)(2,1)} async-done(((bf16[4096,128]{1,0:T(8,128)(2,1)}), bf16[4096,2048]{1,0:T(8,128)(2,1)}) %all-gather.30.cloned.1.call-update) | async-done | bytes 16777232 | tf_op jit(solution)/shard_map/all_gather | solution.py:60
  907.9 13.2 multiply_convert_fusion.3
  933.4 13.1 multiply_convert_fusion.5
  982.6 106.5 %all-reduce.18.cloned.1.call-done = (f32[256,2048]{1,0:T(8,128)}, f32[256,2048]{1,0:T(8,128)}) async-done(((f32[256,2048]{1,0:T(8,128)}, f32[256,2048]{1,0:T(8,128)}), (f32[256,2048]{1,0:T(8,128)}, f32[256,2048]{1,0:T(8,128)})) %all-reduce.18.cloned.1.call-update) | async-done | bytes 4194320 | tf_op jit(solution)/shard_map/psum | solution.py:196
  1137.9 13.7 multiply_reduce_fusion.1
  1236.0 29.5 %reduce-scatter.18.cloned.1.call-done = bf16[256,1024]{0,1:T(8,128)(2,1)} async-done(((bf16[1024,1024]{0,1:T(8,128)(2,1)}), bf16[256,1024]{0,1:T(8,128)(2,1)}) %reduce-scatter.18.cloned.1.call-update) | async-done | bytes 524304 | tf_op jit(solution)/shard_map/reduce_scatter | solution.py:234
  1273.6 37.5 %reduce-scatter.14.cloned.1.call-done = bf16[256,1024]{0,1:T(8,128)(2,1)} async-done(((bf16[1024,1024]{0,1:T(8,128)(2,1)}), bf16[256,1024]{0,1:T(8,128)(2,1)}) %reduce-scatter.14.cloned.1.call-update) | async-done | bytes 524304 | tf_op jit(solution)/shard_map/reduce_scatter | solution.py:234
  1347.4 15.1 fusion.144
  1362.5 25.4 convolution_add_fusion.2
  1388.0 15.2 fusion.145
  1403.2 25.0 convolution_add_fusion.1
  1428.6 21.1 fusion.56
  1449.7 22.7 convolution_add_fusion
  1477.7 63.2 %all-reduce.10 = (f32[2048]{0:T(1024)S(1)}, f32[2048]{0:T(1024)S(1)}) all-reduce(f32[2048]{0:T(1024)S(1)} %add.260, f32[2048]{0:T(1024)S(1)} %add.265), channel_id=6, replica_groups=mesh['fsdp'=4,'ctx'=4,'tensor'=2] {'fsdp','ctx'}, use_global_device_ids=true, to_apply=%region_32.33.clone | all-reduce | flops 4096 | bytes 32768
  1552.3 93.6 %reduce-scatter.20.cloned.1.call-done = f32[128,1024]{1,0:T(8,128)} async-done(((f32[2048,1024]{1,0:T(8,128)}), f32[128,1024]{1,0:T(8,128)}) %reduce-scatter.20.cloned.1.call-update) | async-done | bytes 524304 | tf_op jit(solution)/shard_map/reduce_scatter | solution.py:67
  1645.9 109.6 %reduce-scatter.22.cloned.1.call-done = f32[128,1024]{1,0:T(8,128)} async-done(((f32[2048,1024]{1,0:T(8,128)}), f32[128,1024]{1,0:T(8,128)}) %reduce-scatter.22.cloned.1.call-update) | async-done | bytes 524304 | tf_op jit(solution)/shard_map/reduce_scatter | solution.py:68
  1755.6 109.5 %reduce-scatter.24.cloned.1.call-done = f32[128,1024]{1,0:T(8,128)} async-done(((f32[2048,1024]{1,0:T(8,128)}), f32[128,1024]{1,0:T(8,128)}) %reduce-scatter.24.cloned.1.call-update) | async-done | bytes 524304 | tf_op jit(solution)/shard_map/reduce_scatter | solution.py:69
  1865.1 337.9 %reduce-scatter.28.cloned.1.call-done = f32[128,4096]{1,0:T(8,128)} async-done(((f32[2048,4096]{1,0:T(8,128)}), f32[128,4096]{1,0:T(8,128)}) %reduce-scatter.28.cloned.1.call-update) | async-done | bytes 2097168 | tf_op jit(solution)/shard_map/reduce_scatter | solution.py:77
  2203.0 337.0 %reduce-scatter.30.cloned.1.call-done = f32[128,4096]{1,0:T(8,128)} async-done(((f32[2048,4096]{1,0:T(8,128)}), f32[128,4096]{1,0:T(8,128)}) %reduce-scatter.30.cloned.1.call-update) | async-done | bytes 2097168 | tf_op jit(solution)/shard_map/reduce_scatter | solution.py:78
  2540.0 337.2 %reduce-scatter.32.cloned.1.call-done = f32[4096,128]{1,0:T(8,128)} async-done(((f32[4096,2048]{1,0:T(8,128)}), f32[4096,128]{1,0:T(8,128)}) %reduce-scatter.32.cloned.1.call-update) | async-done | bytes 2097168 | tf_op jit(solution)/shard_map/reduce_scatter | solution.py:79
  (357 shorter events, 399.3 us)
Async XLA Ops:
  7.2 56.3 %all-gather.18.cloned.1.call-start = ((), (), s32[]{:S(2)}) async-start(), calls=%async_computation.13 | async-start | bytes 4456448 | tf_op jit(solution)/shard_map/all_gather | solution.py:48
  7.9 107.1 %all-gather.20.cloned.1.call-start = ((), (), s32[]{:S(2)}) async-start(), calls=%async_computation.14 | async-start | bytes 4456448 | tf_op jit(solution)/shard_map/all_gather | solution.py:49
  8.7 157.8 %all-gather.14.cloned.1.call-start = ((), (), s32[]{:S(2)}) async-start(), calls=%async_computation.11 | async-start | bytes 4456448 | tf_op jit(solution)/shard_map/all_gather | solution.py:50
  9.4 203.8 %all-gather.34.cloned.1.call-start = ((), (), s32[]{:S(2)}) async-start(), calls=%async_computation.21 | async-start | bytes 2621440 | tf_op jit(solution)/shard_map/all_gather | solution.py:141
  43.3 134.3 %copy-start.58 = (f32[16,1,128]{2,1,0:T(1,128)}, f32[16,1,128]{2,1,0:T(1,128)S(1)}, u32[]{:S(2)}) copy-start(f32[16,1,128]{2,1,0:T(1,128)S(1)} %convert_element_type.336) | copy-start | bytes 24580
  51.6 121.3 %copy-start.76 = (f32[256]{0:T(256)}, f32[256]{0:T(256)S(1)}, u32[]{:S(2)}) copy-start(f32[256]{0:T(256)S(1)} %fusion.105) | copy-start | bytes 3076
  128.2 131.5 %all-gather.22.cloned.1.call-start = ((), (), s32[]{:S(2)}) async-start(), calls=%async_computation.15 | async-start | bytes 2621440 | tf_op jit(solution)/shard_map/all_gather | solution.py:141
  134.5 125.2 %copy-start.42 = (bf16[256,16,32]{0,2,1:T(8,128)(2,1)}, bf16[256,16,32]{0,2,1:T(8,128)(2,1)S(1)}, u32[]{:S(2)}) copy-start(bf16[256,16,32]{0,2,1:T(8,128)(2,1)S(1)} %get-tuple-element.57) | copy-start | bytes 786436
  135.4 170.8 %all-gather.32.cloned.1.call-start = ((), (), s32[]{:S(2)}) async-start(), calls=%async_computation.20 | async-start | bytes 2621440 | tf_op jit(solution)/shard_map/all_gather | solution.py:142
  177.5 175.3 %all-gather.16.cloned.1.call-start = ((), (), s32[]{:S(2)}) async-start(), calls=%async_computation.12 | async-start | bytes 2621440 | tf_op jit(solution)/shard_map/all_gather | solution.py:142
  182.0 224.4 %all-gather.24.cloned.1.call-start = ((), (), s32[]{:S(2)}) async-start(), calls=%async_computation.16 | async-start | bytes 4456448 | tf_op jit(solution)/shard_map/all_gather | solution.py:51
  182.7 337.8 %all-reduce.20.cloned.1.call-start = ((), (), s32[]{:S(2)}) async-start(), calls=%async_computation.34 | async-start | bytes 8388608 | tf_op jit(solution)/shard_map/psum | solution.py:154
  183.8 122.4 %copy-start.28 = (pred[256,1024]{1,0:T(8,128)(4,1)}, pred[256,1024]{1,0:T(8,128)(4,1)S(1)}, u32[]{:S(2)}) copy-start(pred[256,1024]{1,0:T(8,128)(4,1)S(1)} %get-tuple-element.88) | copy-start | bytes 786436
  414.0 235.7 %all-gather.26.cloned.1.call-start = ((), (), s32[]{:S(2)}) async-start(), calls=%async_computation.17 | async-start | bytes 17825792 | tf_op jit(solution)/shard_map/all_gather | solution.py:58
  414.6 362.7 %all-gather.28.cloned.1.call-start = ((), (), s32[]{:S(2)}) async-start(), calls=%async_computation.18 | async-start | bytes 17825792 | tf_op jit(solution)/shard_map/all_gather | solution.py:59
  415.3 492.6 %all-gather.30.cloned.1.call-start = ((), (), s32[]{:S(2)}) async-start(), calls=%async_computation.19 | async-start | bytes 17825792 | tf_op jit(solution)/shard_map/all_gather | solution.py:60
  415.9 673.3 %all-reduce.18.cloned.1.call-start = ((), (), s32[]{:S(2)}) async-start(), calls=%async_computation.33 | async-start | bytes 8388608 | tf_op jit(solution)/shard_map/psum | solution.py:196
  525.7 251.5 %copy-start.19 = (bf16[256,2048]{1,0:T(8,128)(2,1)}, bf16[256,2048]{1,0:T(8,128)(2,1)S(1)}, u32[]{:S(2)}) copy-start(bf16[256,2048]{1,0:T(8,128)(2,1)S(1)} %get-tuple-element.76) | copy-start | bytes 3145732
  525.8 270.6 %copy-start.17 = (bf16[256,2048]{1,0:T(8,128)(2,1)}, bf16[256,2048]{1,0:T(8,128)(2,1)S(1)}, u32[]{:S(2)}) copy-start(bf16[256,2048]{1,0:T(8,128)(2,1)S(1)} %get-tuple-element.75) | copy-start | bytes 3145732
  796.3 111.6 %copy-start.22 = (bf16[2,256,2048]{2,1,0:T(8,128)(2,1)S(1)}, bf16[2,256,2048]{2,1,0:T(8,128)(2,1)}, u32[]{:S(2)}) copy-start(bf16[2,256,2048]{2,1,0:T(8,128)(2,1)} %param.14) | copy-start | bytes 6291460
  982.6 239.8 %reduce-scatter.16.cloned.1.call-start = ((), (), s32[]{:S(2)}) async-start(), calls=%async_computation.24 | async-start | bytes 2621440 | tf_op jit(solution)/shard_map/reduce_scatter | solution.py:228
  1130.8 92.8 %reduce-scatter.12.cloned.1.call-start = ((), (), s32[]{:S(2)}) async-start(), calls=%async_computation.22 | async-start | bytes 2621440 | tf_op jit(solution)/shard_map/reduce_scatter | solution.py:228
  1167.9 97.7 %reduce-scatter.18.cloned.1.call-start = ((), (), s32[]{:S(2)}) async-start(), calls=%async_computation.25 | async-start | bytes 2621440 | tf_op jit(solution)/shard_map/reduce_scatter | solution.py:234
  1178.9 132.2 %reduce-scatter.14.cloned.1.call-start = ((), (), s32[]{:S(2)}) async-start(), calls=%async_computation.23 | async-start | bytes 2621440 | tf_op jit(solution)/shard_map/reduce_scatter | solution.py:234
  1207.0 267.3 %all-reduce.22.cloned.1.call-start = ((), (), s32[]{:S(2)}) async-start(), calls=%async_computation.35 | async-start | bytes 8388608 | tf_op jit(solution)/shard_map/psum | solution.py:165
  1316.6 235.7 %reduce-scatter.26.cloned.1.call-start = ((), (), s32[]{:S(2)}) async-start(), calls=%async_computation.29 | async-start | bytes 8912896 | tf_op jit(solution)/shard_map/reduce_scatter | solution.py:70
  1323.9 322.0 %reduce-scatter.20.cloned.1.call-start = ((), (), s32[]{:S(2)}) async-start(), calls=%async_computation.26 | async-start | bytes 8912896 | tf_op jit(solution)/shard_map/reduce_scatter | solution.py:67
  1332.8 422.7 %reduce-scatter.22.cloned.1.call-start = ((), (), s32[]{:S(2)}) async-start(), calls=%async_computation.27 | async-start | bytes 8912896 | tf_op jit(solution)/shard_map/reduce_scatter | solution.py:68
  1339.1 526.0 %reduce-scatter.24.cloned.1.call-start = ((), (), s32[]{:S(2)}) async-start(), calls=%async_computation.28 | async-start | bytes 8912896 | tf_op jit(solution)/shard_map/reduce_scatter | solution.py:69
  1346.2 856.7 %reduce-scatter.28.cloned.1.call-start = ((), (), s32[]{:S(2)}) async-start(), calls=%async_computation.30 | async-start | bytes 35651584 | tf_op jit(solution)/shard_map/reduce_scatter | solution.py:77
  1387.9 1152.1 %reduce-scatter.30.cloned.1.call-start = ((), (), s32[]{:S(2)}) async-start(), calls=%async_computation.31 | async-start | bytes 35651584 | tf_op jit(solution)/shard_map/reduce_scatter | solution.py:78
  1428.3 1448.9 %reduce-scatter.32.cloned.1.call-start = ((), (), s32[]{:S(2)}) async-start(), calls=%async_computation.32 | async-start | bytes 35651584 | tf_op jit(solution)/shard_map/reduce_scatter | solution.py:79
  (86 other events, 1533.0 us)
Sparse Core Ops, SparseCore 0:
  10.2 53.2 all-gather.17
  65.7 49.2 all-gather.19
  117.2 49.1 all-gather.13
  168.5 44.7 all-gather.33
  215.2 44.4 all-gather.21
  261.7 44.4 all-gather.31
  308.3 44.4 all-gather.15
  354.9 51.4 all-gather.23
  414.1 106.3 all-reduce.19
  522.8 126.8 all-gather.25
  652.2 125.0 all-gather.27
  779.4 128.5 all-gather.29
  982.7 106.3 all-reduce.17
  1130.9 43.8 reduce-scatter.15
  1177.0 43.1 reduce-scatter.11
  1222.4 43.1 reduce-scatter.17
  1267.8 43.2 reduce-scatter.13
  1316.8 108.2 all-reduce.21
  1430.3 106.2 reduce-scatter.25
  1541.6 104.2 reduce-scatter.19
  1651.1 104.4 reduce-scatter.21
  1760.8 104.2 reduce-scatter.23
  1870.5 332.4 reduce-scatter.27
  2208.3 331.7 reduce-scatter.29
  2545.4 331.7 reduce-scatter.31
where the time goes:
time: 2890 us; the launch traced here: 2880 us
  waiting for transfers between devices  2190 us (76%)
  matrix products  429 us (15%)
  blocking collectives  127 us (4%)
  other arithmetic  66 us (2%)
  local copies, waits for them, and re-layouts  50.1 us (2%)
    reduce_scatter x1, waiting for transfers between devices, settle_feedforward(): lax.psum_scatter(parts[1], ('fsdp', 'ctx'), scatter_dimension=0, tiled=True)  338 us
    reduce_scatter x1, waiting for transfers between devices, settle_feedforward(): lax.psum_scatter(parts[3], ('fsdp', 'ctx'), scatter_dimension=1, tiled=True)  337 us
    reduce_scatter x1, waiting for transfers between devices, settle_feedforward(): lax.psum_scatter(parts[2], ('fsdp', 'ctx'), scatter_dimension=0, tiled=True)  337 us
    all_gather x1, waiting for transfers between devices, fetch_feedforward(): lax.all_gather(w_gate, ('fsdp', 'ctx'), axis=0, tiled=True)  124 us
    all_gather x1, waiting for transfers between devices, fetch_feedforward(): lax.all_gather(w_up, ('fsdp', 'ctx'), axis=0, tiled=True)  117 us
    reduce_scatter x1, waiting for transfers between devices, settle_attention(): lax.psum_scatter(parts[2], ('fsdp', 'ctx'), scatter_dimension=0, tiled=True)  110 us
    reduce_scatter x1, waiting for transfers between devices, settle_attention(): lax.psum_scatter(parts[3], ('fsdp', 'ctx'), scatter_dimension=0, tiled=True)  110 us
    psum x1, waiting for transfers between devices, per_device(): back_two = lax.psum(back_two, 'tensor')  107 us
  transfers between devices with their start and end apart: 25, of which 21 were waited for; matrix products, arithmetic and copies ran while one was open for 14% of the time, Pallas kernels for 0%

commit v1 on v0

v1 whole, which is shorter than its diff:
```python
import functools

import jax
import jax.numpy as jnp
from jax import lax
from jax.experimental import pallas as pl
from jax.experimental.pallas import tpu as pltpu
from jax.sharding import Mesh
from jax.sharding import PartitionSpec as P

HEAD_DIM = 64
HALF = HEAD_DIM // 2
PAIR = 2 * HEAD_DIM
NORM_EPS = 1e-05
ROPE_BASE = 130000.0
MASKED = -1e30
Q_BLOCK = 256
MLP_CHUNKS = 2
BF16 = jnp.bfloat16
F32 = jnp.float32


def rms_scale(values, gain):
    return values * lax.rsqrt(jnp.mean(values * values, axis=-1, keepdims=True) + NORM_EPS) * gain


def doc_starts(segment_ids):
    places = jnp.arange(segment_ids.shape[0], dtype=jnp.int32)
    before = jnp.concatenate([segment_ids[:1] - 1, segment_ids[:-1]])
    starts = jnp.where(segment_ids != before, places, jnp.zeros_like(places))
    return lax.cummax(starts, axis=0)


def rope_tables(starts):
    places = jnp.arange(starts.shape[0], dtype=jnp.int32)
    lanes = jnp.arange(PAIR, dtype=jnp.int32)
    frequency = ROPE_BASE ** (-(lanes % HALF).astype(F32) * 2.0 / HEAD_DIM)
    angles = (places - starts).astype(F32)[:, None] * frequency[None, :]
    sign = jnp.where(lanes % HEAD_DIM < HALF, -1.0, 1.0).astype(F32)
    return jnp.cos(angles), jnp.sin(angles) * sign[None, :]


def dot(left, right, contract):
    return lax.dot_general(left, right, (contract, ((), ())), preferred_element_type=F32)


def swap_halves(values):
    lanes = lax.broadcasted_iota(jnp.int32, values.shape, 1)
    return jnp.where(
        lanes % HEAD_DIM < HALF,
        pltpu.roll(values, PAIR - HALF, 1),
        pltpu.roll(values, HALF, 1),
    )


def head_lanes(values, head):
    lanes = lax.broadcasted_iota(jnp.int32, values.shape, 1)
    return jnp.where(lanes // HEAD_DIM == head, values, 0.0)


def block_scores(query, keys, starts, row):
    scores = dot(query, keys, ((1,), (1,)))
    cols = lax.broadcasted_iota(jnp.int32, scores.shape, 1)
    rows = lax.broadcasted_iota(jnp.int32, scores.shape, 0) + row
    return jnp.where((cols >= starts) & (cols <= rows), scores, MASKED)


def attention_forward(q_ref, k_ref, v_ref, cos_ref, sin_ref, start_ref, o_ref, lse_ref, km, vm):
    length = q_ref.shape[0]
    cosine, sine = cos_ref[...], sin_ref[...]
    query = q_ref[...] * cosine + swap_halves(q_ref[...]) * sine
    query = query.astype(BF16) * jnp.asarray(0.125, BF16)
    keys = k_ref[...] * cosine + swap_halves(k_ref[...]) * sine
    for head in range(2):
        km[head] = head_lanes(keys, head).astype(BF16)
        vm[head] = head_lanes(v_ref[...], head).astype(BF16)
    for row in range(0, length, Q_BLOCK):
        end = row + Q_BLOCK
        total = jnp.zeros((Q_BLOCK, PAIR), F32)
        logs = jnp.zeros((Q_BLOCK, PAIR), F32)
        lanes = lax.broadcasted_iota(jnp.int32, (Q_BLOCK, PAIR), 1)
        for head in range(2):
            scores = block_scores(
                query[row:end], km[head, :end], start_ref[row:end, :1], row
            )
            peak = jnp.max(scores, axis=-1, keepdims=True)
            weights = jnp.exp(scores - peak)
            weight_sum = jnp.sum(weights, axis=-1, keepdims=True)
            weights = (weights * (1.0 / weight_sum)).astype(BF16)
            total = total + dot(weights, vm[head, :end], ((1,), (0,)))
            logs = jnp.where(lanes // HEAD_DIM == head, peak + jnp.log(weight_sum), logs)
        o_ref[row:end] = total.astype(BF16)
        lse_ref[row:end] = logs


def attention_backward(
    q_ref, k_ref, v_ref, do_ref, lse_ref, cos_ref, sin_ref, start_ref, d_ref, km, qm, vm, dom, dq, dk, dv
):
    part = pl.program_id(1)
    length = q_ref.shape[0]

    @pl.when(part == 0)
    def _():
        cosine, sine = cos_ref[...], sin_ref[...]
        query = q_ref[...] * cosine + swap_halves(q_ref[...]) * sine
        keys = k_ref[...] * cosine + swap_halves(k_ref[...]) * sine
        grads = do_ref[...].astype(F32)
        for head in range(2):
            km[head] = head_lanes(keys, head).astype(BF16)
            qm[head] = head_lanes(query, head).astype(BF16) * jnp.asarray(0.125, BF16)
            vm[head] = head_lanes(v_ref[...], head).astype(BF16)
            dom[head] = head_lanes(grads, head).astype(BF16)
        dk[...] = jnp.zeros_like(dk)
        dv[...] = jnp.zeros_like(dv)
        for row in range(0, length, Q_BLOCK):
            end = row + Q_BLOCK
            dq_block = jnp.zeros((Q_BLOCK, PAIR), F32)
            for head in range(2):
                scores = block_scores(
                    qm[head, row:end], km[head, :end], start_ref[row:end, :1], row
                )
                lse = lse_ref[row:end, head * HEAD_DIM : head * HEAD_DIM + 1]
                probs = jnp.exp(scores - lse)
                probs_grad = dot(dom[head, row:end], vm[head, :end], ((1,), (1,)))
                inner = jnp.sum(probs * probs_grad, axis=-1, keepdims=True)
                scores_grad = (probs * (probs_grad - inner)).astype(BF16)
                dq_block = dq_block + dot(scores_grad, km[head, :end], ((1,), (0,)))
                dk[:end] += dot(scores_grad, qm[head, row:end], ((0,), (0,)))
                dv[:end] += dot(probs.astype(BF16), dom[head, row:end], ((0,), (0,)))
            dq[row:end] = dq_block
        grad = dq[...] * 0.125
        d_ref[...] = (grad * cosine - swap_halves(grad) * sine).astype(BF16)

    @pl.when(part == 1)
    def _():
        grad = dk[...].astype(BF16).astype(F32)
        d_ref[...] = (grad * cos_ref[...] - swap_halves(grad) * sin_ref[...]).astype(BF16)

    @pl.when(part == 2)
    def _():
        d_ref[...] = dv[...].astype(BF16)


def run_attention_forward(qkv, cosine, sine, starts):
    length, pairs = qkv.shape[0], qkv.shape[1] // (3 * PAIR)
    column = lambda offset: pl.BlockSpec((length, PAIR), lambda p: (0, offset + p))
    whole = pl.BlockSpec((length, PAIR), lambda p: (0, 0))
    return pl.pallas_call(
        attention_forward,
        grid=(pairs,),
        in_specs=[column(0), column(pairs), column(2 * pairs), whole, whole, whole],
        out_specs=[column(0), column(0)],
        out_shape=[
            jax.ShapeDtypeStruct((length, pairs * PAIR), BF16),
            jax.ShapeDtypeStruct((length, pairs * PAIR), F32),
        ],
        scratch_shapes=[pltpu.VMEM((2, length, PAIR), BF16)] * 2,
        compiler_params=pltpu.CompilerParams(vmem_limit_bytes=48 * 2**20),
        name="attention_forward",
    )(qkv, qkv, qkv, cosine, sine, starts)


def run_attention_backward(qkv, grads, logs, cosine, sine, starts):
    length, pairs = qkv.shape[0], qkv.shape[1] // (3 * PAIR)
    column = lambda offset: pl.BlockSpec((length, PAIR), lambda p, part: (0, offset + p))
    whole = pl.BlockSpec((length, PAIR), lambda p, part: (0, 0))
    return pl.pallas_call(
        attention_backward,
        grid=(pairs, 3),
        in_specs=[
            column(0), column(pairs), column(2 * pairs), column(0), column(0), whole, whole, whole,
        ],
        out_specs=pl.BlockSpec((length, PAIR), lambda p, part: (0, part * pairs + p)),
        out_shape=jax.ShapeDtypeStruct((length, 3 * pairs * PAIR), BF16),
        scratch_shapes=[pltpu.VMEM((2, length, PAIR), BF16)] * 4
        + [pltpu.VMEM((length, PAIR), F32)] * 3,
        compiler_params=pltpu.CompilerParams(vmem_limit_bytes=48 * 2**20),
        name="attention_backward",
    )(qkv, qkv, qkv, grads, logs, cosine, sine, starts)


def swap(values, axis, size, step):
    return lax.ppermute(values, axis, [(i, i ^ step) for i in range(size)])


def by_index(parts, index):
    parts = list(parts)
    bit = 1
    while bit < len(parts):
        odd = (index & bit) != 0
        parts = [jnp.where(odd, parts[j ^ bit], parts[j]) for j in range(len(parts))]
        bit *= 2
    return parts


def per_device(
    sizes, tokens, segments, cotangent, attn_gain, w_query, w_key, w_value, w_out, mlp_gain, w_gate, w_up, w_down
):
    ny, nc, nx = sizes
    nq = ny * nx
    yi, core, ctx, xi = (lax.axis_index(name) for name in ("y", "core", "ctx", "tensor"))
    quarter = yi * nx + xi
    group = ("y", "tensor")
    batch, chunk, width = tokens.shape
    length = segments.shape[1]
    piece_rows = chunk // nq
    rows = w_query.shape[0]

    def pick(array, index, axis):
        return lax.dynamic_index_in_dim(array, index, axis, keepdims=False)

    def permuted(values):
        lead = values.shape[:-1]
        return values.reshape(lead + (ny, 2 * nc, rows)).swapaxes(-3, -2).reshape(lead + (width,))

    def unpermuted(values):
        lead = values.shape[:-1]
        return values.reshape(lead + (2 * nc, ny, rows)).swapaxes(-3, -2).reshape(lead + (width,))

    def pieces_in(values):
        values = permuted(values).reshape(batch, nq, piece_rows, width)
        parts = [pick(values, quarter, 1)]
        for step in range(1, ny):
            parts.append(swap(pick(values, (yi ^ step) * nx + xi, 1), "y", ny, step))
        ordered = jnp.concatenate(by_index(parts, yi), axis=0)
        return lax.all_to_all(ordered, "ctx", 0, 0, tiled=True)

    def pieces_out(piece):
        held = lax.all_to_all(piece, "ctx", 0, 0, tiled=True)
        held = held.reshape(ny, batch, piece_rows, width)
        parts = [pick(held, yi, 0)]
        for step in range(1, nq):
            parts.append(swap(pick(held, (quarter ^ step) // nx, 0), group, nq, step))
        ordered = jnp.stack(by_index(parts, quarter), axis=1)
        return unpermuted(ordered.reshape(batch, chunk, width))

    def gather_rows(piece):
        out = jnp.zeros((nc, nq, piece_rows, width), piece.dtype)
        for step in range(nq):
            part = piece if step == 0 else swap(piece, group, nq, step)
            out = lax.dynamic_update_slice(out, part[:, None], (0, quarter ^ step, 0, 0))
        return out.reshape(length, width)

    def sum_rows(partial):
        partial = partial.reshape(nc, nq, piece_rows, width)
        total = pick(partial, quarter, 1).astype(F32)
        for step in range(1, nq):
            total = total + swap(pick(partial, quarter ^ step, 1), group, nq, step).astype(F32)
        return total

    def fetch(blocks):
        parts = [blocks(yi)]
        for step in range(1, ny):
            parts.append(swap(blocks(yi ^ step), "y", ny, step))
        held = jnp.concatenate(by_index(parts, yi), axis=0)
        return lax.all_gather(held, ("core", "ctx"), axis=0, tiled=True)

    def columns(weight, index, start, count):
        share = weight.shape[1] // ny
        return lax.dynamic_slice_in_dim(weight, index * share + start, count, axis=1)

    def settle(left, right):
        half = width // 2
        other = lax.dynamic_slice_in_dim(left, (1 - core) * half, half, axis=1)
        mine = lax.dynamic_slice_in_dim(left, core * half, half, axis=1)
        away = dot(other, right, ((0,), (0,))).astype(BF16)
        came = swap(away, "core", 2, 1)
        held = (dot(mine, right, ((0,), (0,))) + came.astype(F32)).astype(BF16)
        return lax.psum_scatter(held, "ctx", scatter_dimension=0, tiled=True)

    def own_rows(summed):
        summed = summed.reshape(ny, rows, -1)
        parts = [pick(summed, yi, 0)]
        for step in range(1, ny):
            parts.append(swap(pick(summed, yi ^ step, 0), "y", ny, step))
        return by_index(parts, yi)

    gains = lax.all_gather(
        jnp.concatenate([attn_gain, mlp_gain])[None], ("core", "ctx", "y"), axis=0, tiled=True
    )
    gain_one = gains[:, :rows].reshape(width).astype(F32)
    gain_two = gains[:, rows:].reshape(width).astype(F32)

    head_cols = w_query.shape[1] // ny
    qkv_weight = fetch(
        lambda index: jnp.concatenate(
            [columns(w, index, 0, head_cols) for w in (w_query, w_key, w_value)], axis=1
        )
    )
    out_turned = w_out.T
    out_weight = fetch(lambda index: columns(out_turned, index, 0, head_cols))

    seg_parts = [segments] + [swap(segments, "y", ny, step) for step in range(1, ny)]
    all_segments = jnp.concatenate(by_index(seg_parts, yi), axis=0)
    starts = doc_starts(pick(all_segments, ctx, 0))
    cosine, sine = rope_tables(starts)
    starts = jnp.broadcast_to(starts[:, None], (length, PAIR))

    x_piece = pieces_in(tokens).astype(F32)
    normed = gather_rows(rms_scale(x_piece, gain_one).astype(BF16))
    up_piece = pieces_in(cotangent)
    upstream = gather_rows(up_piece)

    hidden_cols = w_gate.shape[1] // ny
    part_cols = hidden_cols // MLP_CHUNKS
    down_turned = w_down.T
    mlp_weights = []
    for part in range(MLP_CHUNKS):
        start = part * part_cols
        gate_up = fetch(
            lambda index: jnp.concatenate(
                [columns(w, index, start, part_cols) for w in (w_gate, w_up)], axis=1
            )
        )
        mlp_weights.append((gate_up, fetch(lambda index: columns(down_turned, index, start, part_cols))))

    qkv = dot(normed, qkv_weight, ((1,), (0,)))
    attended, logs = run_attention_forward(qkv, cosine, sine, starts)
    attn_sum = sum_rows(dot(attended, out_weight, ((1,), (1,))).astype(BF16))
    residual = x_piece + attn_sum
    normed_two = gather_rows(rms_scale(residual, gain_two).astype(BF16))

    mlp_out = None
    back_two = None
    mlp_grads = []
    for gate_up, down in mlp_weights:
        both = dot(normed_two, gate_up, ((1,), (0,)))
        gate, up = both[:, :part_cols], both[:, part_cols:]
        hidden_grad = dot(upstream, down, ((1,), (0,)))
        sigmoid = jax.nn.sigmoid(gate)
        silu = gate * sigmoid
        hidden = (silu * up).astype(BF16)
        gate_grad = hidden_grad * up * (sigmoid + silu * (1.0 - sigmoid))
        both_grad = jnp.concatenate([gate_grad, hidden_grad * silu], axis=1).astype(BF16)
        term = dot(both_grad, gate_up, ((1,), (1,)))
        back_two = term if back_two is None else back_two + term
        term = dot(hidden, down, ((1,), (1,)))
        mlp_out = term if mlp_out is None else mlp_out + term
        mlp_grads.append((settle(normed_two, both_grad), settle(upstream, hidden)))

    back_two = sum_rows(back_two.astype(BF16))
    _, norm_two_back = jax.vjp(rms_scale, residual, gain_two)
    residual_grad, gain_two_grad = norm_two_back(back_two)
    residual_grad = residual_grad + up_piece.astype(F32)
    residual_low = gather_rows(residual_grad.astype(BF16))
    attended_grad = dot(residual_low, out_weight, ((1,), (0,))).astype(BF16)
    out_grad = settle(residual_low, attended)

    qkv_grad = run_attention_backward(qkv, attended_grad, logs, cosine, sine, starts)
    back_one = sum_rows(dot(qkv_grad, qkv_weight, ((1,), (1,))).astype(BF16))
    qkv_weight_grad = settle(normed, qkv_grad)
    _, norm_one_back = jax.vjp(rms_scale, x_piece, gain_one)
    inputs_grad, gain_one_grad = norm_one_back(back_one)
    grad_tokens = pieces_out((inputs_grad + residual_grad).astype(BF16)).astype(F32)
    block_out = pieces_out((residual + sum_rows(mlp_out.astype(BF16))).astype(BF16))

    gain_grads = lax.psum(
        jnp.stack([gain_one_grad, gain_two_grad]), ("y", "core", "ctx", "tensor")
    ).reshape(2, 2 * nc * ny, rows)
    gain_grads = pick(gain_grads, (core * nc + ctx) * ny + yi, 1)

    qkv_parts = own_rows(qkv_weight_grad)
    grad_query, grad_key, grad_value = (
        jnp.concatenate(
            [p[:, i * head_cols : (i + 1) * head_cols] for p in qkv_parts], axis=1
        ).astype(F32)
        for i in range(3)
    )
    grad_out = jnp.concatenate(own_rows(out_grad), axis=1).T.astype(F32)
    gate_up_parts = [own_rows(pair[0]) for pair in mlp_grads]
    down_parts = [own_rows(pair[1]) for pair in mlp_grads]
    grad_gate, grad_up = (
        jnp.concatenate(
            [p[y][:, i * part_cols : (i + 1) * part_cols] for y in range(ny) for p in gate_up_parts],
            axis=1,
        ).astype(F32)
        for i in range(2)
    )
    grad_down = jnp.concatenate([p[y] for y in range(ny) for p in down_parts], axis=1).T.astype(F32)
    return (
        block_out,
        grad_tokens,
        gain_grads[0],
        grad_query,
        grad_key,
        grad_value,
        grad_out,
        gain_grads[1],
        grad_gate,
        grad_up,
        grad_down,
    )


def solution(mesh):
    ny, nc, nx = mesh.shape["fsdp"] // 2, mesh.shape["ctx"], mesh.shape["tensor"]
    fine = Mesh(mesh.devices.reshape(ny, 2, nc, nx), ("y", "core", "ctx", "tensor"))
    fsdp = ("y", "core")
    owner = ("y", "core", "ctx")
    token_spec = P(fsdp, "ctx", None)
    weight_specs = (
        P(owner),
        P(owner, "tensor"),
        P(owner, "tensor"),
        P(owner, "tensor"),
        P("tensor", owner),
        P(owner),
        P(owner, "tensor"),
        P(owner, "tensor"),
        P("tensor", owner),
    )
    return jax.shard_map(
        functools.partial(per_device, (ny, nc, nx)),
        mesh=fine,
        in_specs=(token_spec, P(fsdp, None), token_spec) + weight_specs,
        out_specs=(token_spec, token_spec) + weight_specs,
        check_vma=False,
    )
```

time: 2890 us -> 1070 us (0.37)
  waiting for transfers between devices: 2190 us -> 464 us
  matrix products: 429 us -> 203 us
  starting transfers between devices: 2.52 us -> 68.7 us
  Pallas kernels: 0 us -> 53.3 us
  local copies, waits for them, and re-layouts: 50.1 us -> 103 us
    reduce_scatter x11 -> x6, waiting for transfers between devices: 1390 us -> 0.07 us  [settle(): return lax.psum_scatter(held, 'ctx', scatter_dimension=0, tiled=True)]
    all_gather x11 -> x6, waiting for transfers between devices: 615 us -> 0.03 us  [fetch(): return lax.all_gather(held, ('core', 'ctx'), axis=0, tiled=True)]
    ppermute x0 -> x51, waiting for transfers between devices: none -> 424 us  [swap(): return lax.ppermute(values, axis, [(i, i ^ step) for i in range(size)])]
    dot_general x54 -> x24, matrix products: 429 us -> 203 us  [dot(): lax.dot_general(left, right, (contract, ((), ())), preferred_element_type...]
    psum x3 -> x0, waiting for transfers between devices: 181 us -> none  [the longest x1 107 us: per_device(): back_two = lax.psum(back_two, 'tensor')]
    psum x0 -> x1, blocking collectives: none -> 71 us  [per_device(): lax.psum(jnp.stack([gain_one_grad, gain_two_grad]), ('y', 'core', 'ctx',...]
    unnamed x1 -> x0, blocking collectives: 63.2 us -> none
    pallas_call x0 -> x2, Pallas kernels: none -> 53.3 us  [the longest x1 34.4 us: run_attention_backward(): pl.pallas_call(attention_backward, grid=(pairs, 3), in_specs=[column(0),...]
  transfers between devices with their start and end apart: 25 -> 67, of which waited for: 21 -> 35; matrix products, arithmetic and copies ran while one was open for 14% -> 27% of each run, Pallas kernels for 0% -> 5%
where the time goes in v1:
time: 1070 us; the launch traced here: 1060 us
  waiting for transfers between devices  464 us (43%)
  matrix products  203 us (19%)
  blocking collectives  111 us (10%)
  local copies, waits for them, and re-layouts  103 us (10%)
  starting transfers between devices  68.7 us (6%)
  Pallas kernels  53.3 us (5%)
  other arithmetic  43.5 us (4%)
  between operations  16.3 us (2%)
    ppermute x51, waiting for transfers between devices, swap(): return lax.ppermute(values, axis, [(i, i ^ step) for i in range(size)])  424 us
    dot_general x24, matrix products, dot(): lax.dot_general(left, right, (contract, ((), ())), preferred_element_type...  203 us
    psum x1, blocking collectives, per_device(): lax.psum(jnp.stack([gain_one_grad, gain_two_grad]), ('y', 'core', 'ctx',...  71 us
    ppermute x51, starting transfers between devices, swap(): return lax.ppermute(values, axis, [(i, i ^ step) for i in range(size)])  52.5 us
    all_gather x1, blocking collectives, per_device(): lax.all_gather(jnp.concatenate([attn_gain, mlp_gain])[None], ('core', 'ct...  40.4 us
    all_to_all x2, waiting for transfers between devices, pieces_out(): held = lax.all_to_all(piece, 'ctx', 0, 0, tiled=True)  39.1 us
    pallas_call x1, Pallas kernels, run_attention_backward(): pl.pallas_call(attention_backward, grid=(pairs, 3), in_specs=[column(0),...  34.4 us
  transfers between devices with their start and end apart: 67, of which 35 were waited for; matrix products, arithmetic and copies ran while one was open for 27% of the time, Pallas kernels for 5%

profile of v1, /device:TPU:0, one launch (start us, length us, event | category | flops | bytes accessed | tf_op | source)
XLA Modules:
  0.0 1063.0 jit_solution(15499432583550142798)
XLA Ops:
  30.8 10.2 collective-permute-done.13
  103.8 40.4 %all-gather.1 = bf16[16,1,256]{2,1,0:T(2,128)(2,1)S(1)} all-gather(bf16[1,1,256]{2,1,0:T(2,128)(2,1)S(1)} %reshape.252), channel_id=2, replica_groups=mesh['y'=2,'core'=2,'ctx'=4,'tensor'=2] {'core','ctx','y'}, dimensions={0}, use_global_device_ids=true | all-gather | bytes 8704 | tf_op jit(solution)/shard_map/all_gather | solution.py:278
  160.7 12.8 %collective-permute-done.1 = bf16[4,64,2048]{2,1,0:T(8,128)(2,1)} collective-permute-done((bf16[4,64,2048]{2,1,0:T(8,128)(2,1)S(1)}, bf16[4,64,2048]{2,1,0:T(8,128)(2,1)}, u32[]{:S(2)}, u32[]{:S(2)}) %collective-permute-start.1) | collective-permute-done | bytes 1048608 | tf_op jit(solution)/shard_map/ppermute | solution.py:183
  175.8 22.8 %collective-permute-done.2 = bf16[4,64,2048]{2,1,0:T(8,128)(2,1)} collective-permute-done((bf16[4,64,2048]{2,1,0:T(8,128)(2,1)S(1)}, bf16[4,64,2048]{2,1,0:T(8,128)(2,1)}, u32[]{:S(2)}, u32[]{:S(2)}) %collective-permute-start.2) | collective-permute-done | bytes 1048608 | tf_op jit(solution)/shard_map/ppermute | solution.py:183
  203.2 11.7 %fusion.81.q_ref.k_ref.v_ref = f32[1024,1536]{1,0:T(8,128)} fusion(bf16[1024,2048]{1,0:T(8,128)(2,1)} %bitcast.345, bf16[2048,1536]{1,0:T(8,128)(2,1)} %all-gather.9.cloned.1.call-done), kind=kOutput, calls=%fused_computation.273 | convolution fusion | flops 6442450944 | bytes 16777216 | tf_op jit(solution)/shard_map/dot_general | solution.py:44
  215.1 18.9 %attention_forward.1 = (bf16[1024,512]{1,0:T(8,128)(2,1)S(1)}, f32[1024,512]{1,0:T(8,128)S(1)}) custom-call(f32[1024,1536]{1,0:T(8,128)} %fusion.81.q_ref.k_ref.v_ref, f32[1024,1536]{1,0:T(8,128)} %fusion.81.q_ref.k_ref.v_ref, f32[1024,1536]{1,0:T(8,128)} %fusion.81.q_ref.k_ref.v_ref, f32[1024,128]{1,0:T(8,128)S(1)} %get-tuple-element.160.cos_ref, ...), custom_call_target="tpu_custom_call" | custom-call | tf_op jit(solution)/shard_map/attention_forward/pallas_call | solution.py:148
  254.0 15.5 %collective-permute-done.7 = bf16[4,64,2048]{2,1,0:T(8,128)(2,1)} collective-permute-done((bf16[4,64,2048]{2,1,0:T(8,128)(2,1)}, bf16[4,64,2048]{2,1,0:T(8,128)(2,1)}, u32[]{:S(2)}, u32[]{:S(2)}) %collective-permute-start.7) | collective-permute-done | bytes 1048608 | tf_op jit(solution)/shard_map/ppermute | solution.py:183
  270.6 22.7 %collective-permute-done.8 = bf16[4,64,2048]{2,1,0:T(8,128)(2,1)} collective-permute-done((bf16[4,64,2048]{2,1,0:T(8,128)(2,1)}, bf16[4,64,2048]{2,1,0:T(8,128)(2,1)}, u32[]{:S(2)}, u32[]{:S(2)}) %collective-permute-start.8) | collective-permute-done | bytes 1048608 | tf_op jit(solution)/shard_map/ppermute | solution.py:183
  300.9 13.5 %collective-permute-done.24 = bf16[4,64,2048]{2,1,0:T(8,128)(2,1)S(1)} collective-permute-done((bf16[4,64,2048]{2,1,0:T(8,128)(2,1)}, bf16[4,64,2048]{2,1,0:T(8,128)(2,1)S(1)}, u32[]{:S(2)}, u32[]{:S(2)}) %collective-permute-start.24) | collective-permute-done | bytes 1048608 | tf_op jit(solution)/shard_map/ppermute | solution.py:183
  315.8 21.0 %collective-permute-done.25 = bf16[4,64,2048]{2,1,0:T(8,128)(2,1)S(1)} collective-permute-done((bf16[4,64,2048]{2,1,0:T(8,128)(2,1)}, bf16[4,64,2048]{2,1,0:T(8,128)(2,1)S(1)}, u32[]{:S(2)}, u32[]{:S(2)}) %collective-permute-start.25) | collective-permute-done | bytes 1048608 | tf_op jit(solution)/shard_map/ppermute | solution.py:183
  338.9 20.5 %collective-permute-done.10 = bf16[4,64,2048]{2,1,0:T(8,128)(2,1)S(1)} collective-permute-done((bf16[4,64,2048]{2,1,0:T(8,128)(2,1)S(1)}, bf16[4,64,2048]{2,1,0:T(8,128)(2,1)S(1)}, u32[]{:S(2)}, u32[]{:S(2)}) %collective-permute-start.10) | collective-permute-done | bytes 1048608 | tf_op jit(solution)/shard_map/ppermute | solution.py:183
  360.5 20.1 %collective-permute-done.11 = bf16[4,64,2048]{2,1,0:T(8,128)(2,1)S(1)} collective-permute-done((bf16[4,64,2048]{2,1,0:T(8,128)(2,1)S(1)}, bf16[4,64,2048]{2,1,0:T(8,128)(2,1)S(1)}, u32[]{:S(2)}, u32[]{:S(2)}) %collective-permute-start.11) | collective-permute-done | bytes 1048608 | tf_op jit(solution)/shard_map/ppermute | solution.py:183
  382.8 14.8 %fusion.82 = f32[1024,2048]{1,0:T(8,128)} fusion(bf16[1024,2048]{1,0:T(8,128)(2,1)} %bitcast.33, bf16[2048,2048]{1,0:T(8,128)(2,1)} %all-gather.13.cloned.1.call-done), kind=kOutput, calls=%fused_computation.274 | convolution fusion | flops 8589934592 | bytes 20971520 | tf_op jit(solution)/shard_map/dot_general | solution.py:44
  397.6 14.5 %multiply_convert_fusion.3 = (bf16[1024,1024]{1,0:T(8,128)(2,1)}, bf16[1024,1024]{1,0:T(8,128)(2,1)}, bf16[1024,1024]{1,0:T(8,128)(2,1)}) fusion(f32[1024,2048]{1,0:T(8,128)} %fusion.82, bf16[1024,2048]{1,0:T(8,128)(2,1)} %bitcast.65, bf16[2048,1024]{0,1:T(8,128)(2,1)} %all-gather.15.cloned.1.call-done), kind=kOutput, calls=%fused_computation.12 | convolution fusion | flops 4309647360 | bytes 23068672 | tf_op jit(solution)/shard_map/dot_general | solution.py:44
  412.1 14.6 %fusion.83 = f32[1024,2048]{1,0:T(8,128)} fusion(bf16[1024,2048]{1,0:T(8,128)(2,1)} %bitcast.33, bf16[2048,2048]{1,0:T(8,128)(2,1)} %all-gather.17.cloned.1.call-done), kind=kOutput, calls=%fused_computation.275 | convolution fusion | flops 8589934592 | bytes 20971520 | tf_op jit(solution)/shard_map/dot_general | solution.py:44
  426.7 13.1 %multiply_convert_fusion.1 = (bf16[1024,1024]{1,0:T(8,128)(2,1)S(1)}, bf16[1024,1024]{1,0:T(8,128)(2,1)S(1)}, bf16[1024,1024]{1,0:T(8,128)(2,1)}) fusion(f32[1024,2048]{1,0:T(8,128)} %fusion.83, bf16[1024,2048]{1,0:T(8,128)(2,1)} %bitcast.65, bf16[2048,1024]{0,1:T(8,128)(2,1)} %all-gather.19.cloned.1.call-done), kind=kOutput, calls=%fused_computation.10 | convolution fusion | flops 4309647360 | bytes 23068672 | tf_op jit(solution)/shard_map/dot_general | solution.py:44
  439.9 11.0 %fusion.38 = f32[1024,2048]{1,0:T(8,128)} fusion(bf16[2048,2048]{1,0:T(8,128)(2,1)S(1)} %copy-done.32, bf16[1024,1024]{1,0:T(8,128)(2,1)S(1)} %get-tuple-element.56, bf16[1024,1024]{1,0:T(8,128)(2,1)S(1)} %get-tuple-element.55), kind=kOutput, calls=%fused_computation.82 | convolution fusion | flops 8598323200 | bytes 20971520 | tf_op jit(solution)/shard_map/dot_general | solution.py:44
  450.9 15.8 %add_convert_fusion.2 = bf16[1024,2048]{1,0:T(8,128)(2,1)} fusion(f32[1024,2048]{1,0:T(8,128)} %fusion.38, bf16[2048,2048]{1,0:T(8,128)(2,1)} %all-gather.13.cloned.1.call-done, bf16[1024,1024]{1,0:T(8,128)(2,1)} %get-tuple-element.54, bf16[1024,1024]{1,0:T(8,128)(2,1)S(1)} %copy-done.40), kind=kOutput, calls=%fused_computation.2 | convolution fusion | flops 8602517504 | bytes 25165824 | tf_op jit(solution)/shard_map/dot_general | solution.py:44
  472.6 22.6 %collective-permute-done.27 = bf16[4,64,2048]{2,1,0:T(8,128)(2,1)S(1)} collective-permute-done((bf16[4,64,2048]{2,1,0:T(8,128)(2,1)S(1)}, bf16[4,64,2048]{2,1,0:T(8,128)(2,1)S(1)}, u32[]{:S(2)}, u32[]{:S(2)}) %collective-permute-start.27) | collective-permute-done | bytes 1048608 | tf_op jit(solution)/shard_map/ppermute | solution.py:183
  495.2 19.0 %collective-permute-done.28 = bf16[4,64,2048]{2,1,0:T(8,128)(2,1)S(1)} collective-permute-done((bf16[4,64,2048]{2,1,0:T(8,128)(2,1)S(1)}, bf16[4,64,2048]{2,1,0:T(8,128)(2,1)S(1)}, u32[]{:S(2)}, u32[]{:S(2)}) %collective-permute-start.28) | collective-permute-done | bytes 1048608 | tf_op jit(solution)/shard_map/ppermute | solution.py:183
  525.6 22.9 %collective-permute-done.30 = bf16[4,64,2048]{2,1,0:T(8,128)(2,1)} collective-permute-done((bf16[4,64,2048]{2,1,0:T(8,128)(2,1)}, bf16[4,64,2048]{2,1,0:T(8,128)(2,1)}, u32[]{:S(2)}, u32[]{:S(2)}) %collective-permute-start.30) | collective-permute-done | bytes 1048608 | tf_op jit(solution)/shard_map/ppermute | solution.py:183
  550.8 16.5 %collective-permute-done.31 = bf16[4,64,2048]{2,1,0:T(8,128)(2,1)} collective-permute-done((bf16[4,64,2048]{2,1,0:T(8,128)(2,1)}, bf16[4,64,2048]{2,1,0:T(8,128)(2,1)}, u32[]{:S(2)}, u32[]{:S(2)}) %collective-permute-start.31) | collective-permute-done | bytes 1048608 | tf_op jit(solution)/shard_map/ppermute | solution.py:183
  611.2 34.4 %attention_backward.1 = bf16[1024,1536]{1,0:T(8,128)(2,1)} custom-call(f32[1024,1536]{1,0:T(8,128)} %fusion.81.q_ref.k_ref.v_ref, f32[1024,1536]{1,0:T(8,128)} %fusion.81.q_ref.k_ref.v_ref, f32[1024,1536]{1,0:T(8,128)} %fusion.81.q_ref.k_ref.v_ref, bf16[1024,512]{1,0:T(8,128)(2,1)S(1)} %convolution_convert_fusion.7.do_ref, f32[1024,512]{1,0:T(8,128)S(1)} %copy-done.3, ...), custom_call_target="tpu_custom_call" | custom-call | tf_op jit(solution)/shard_map/attention_backward/pallas_call | solution.py:167
  685.3 9.6 convolution_convert_fusion.3
  722.2 15.0 %collective-permute-done.33 = bf16[4,64,2048]{2,1,0:T(8,128)(2,1)S(1)} collective-permute-done((bf16[4,64,2048]{2,1,0:T(8,128)(2,1)S(1)}, bf16[4,64,2048]{2,1,0:T(8,128)(2,1)S(1)}, u32[]{:S(2)}, u32[]{:S(2)}) %collective-permute-start.33) | collective-permute-done | bytes 1048608 | tf_op jit(solution)/shard_map/ppermute | solution.py:183
  737.3 22.1 %collective-permute-done.34 = bf16[4,64,2048]{2,1,0:T(8,128)(2,1)S(1)} collective-permute-done((bf16[4,64,2048]{2,1,0:T(8,128)(2,1)S(1)}, bf16[4,64,2048]{2,1,0:T(8,128)(2,1)S(1)}, u32[]{:S(2)}, u32[]{:S(2)}) %collective-permute-start.34) | collective-permute-done | bytes 1048608 | tf_op jit(solution)/shard_map/ppermute | solution.py:183
  762.3 19.9 %collective-permute-done.17 = bf16[4,64,2048]{2,1,0:T(8,128)(2,1)S(1)} collective-permute-done((bf16[4,64,2048]{2,1,0:T(8,128)(2,1)S(1)}, bf16[4,64,2048]{2,1,0:T(8,128)(2,1)S(1)}, u32[]{:S(2)}, u32[]{:S(2)}) %collective-permute-start.17) | collective-permute-done | bytes 1048608 | tf_op jit(solution)/shard_map/ppermute | solution.py:183
  782.2 21.7 %collective-permute-done.18 = bf16[4,64,2048]{2,1,0:T(8,128)(2,1)S(1)} collective-permute-done((bf16[4,64,2048]{2,1,0:T(8,128)(2,1)S(1)}, bf16[4,64,2048]{2,1,0:T(8,128)(2,1)S(1)}, u32[]{:S(2)}, u32[]{:S(2)}) %collective-permute-start.18) | collective-permute-done | bytes 1048608 | tf_op jit(solution)/shard_map/ppermute | solution.py:183
  811.7 10.1 add_convert_fusion
  821.8 39.1 %all-to-all-done.3 = bf16[4,64,2048]{2,1,0:T(8,128)(2,1)S(1)} async-done(((bf16[4,64,2048]{2,1,0:T(8,128)(2,1)}), bf16[4,64,2048]{2,1,0:T(8,128)(2,1)S(1)}, u32[]{:S(2)}, u32[]{:S(2)}) %all-to-all-start.3) | async-done | bytes 1048608 | tf_op jit(solution)/shard_map/all_to_all | solution.py:229
  869.2 71.0 %psum.7 = f32[2,16,128]{2,1,0:T(8,128)S(1)} all-reduce(f32[2,16,128]{2,1,0:T(8,128)S(1)} %bitcast.366), channel_id=1, replica_groups=mesh['y'=2,'core'=2,'ctx'=4,'tensor'=2] {'y','core','ctx','tensor'}, use_global_device_ids=true, to_apply=%region_8.9 | all-reduce | flops 4096 | bytes 32768 | tf_op jit(solution)/shard_map/psum | solution.py:357
  958.0 10.1 collective-permute-done.21
  (365 shorter events, 398.7 us)
Async XLA Ops:
  7.2 196.0 %all-gather.9.cloned.1.call-start = ((), (), s32[]{:S(2)}) async-start(), calls=%async_computation.10 | async-start | bytes 7077888 | tf_op jit(solution)/shard_map/all_gather | solution.py:256
  22.7 213.5 %all-gather.11.cloned.1.call-start = ((), (), s32[]{:S(2)}) async-start(), calls=%async_computation.11 | async-start | bytes 2359296 | tf_op jit(solution)/shard_map/all_gather | solution.py:256
  28.7 354.1 %all-gather.13.cloned.1.call-start = ((), (), s32[]{:S(2)}) async-start(), calls=%async_computation.12 | async-start | bytes 9437184 | tf_op jit(solution)/shard_map/all_gather | solution.py:256
  42.4 355.2 %all-gather.15.cloned.1.call-start = ((), (), s32[]{:S(2)}) async-start(), calls=%async_computation.13 | async-start | bytes 4718592 | tf_op jit(solution)/shard_map/all_gather | solution.py:256
  55.5 356.6 %all-gather.17.cloned.1.call-start = ((), (), s32[]{:S(2)}) async-start(), calls=%async_computation.14 | async-start | bytes 9437184 | tf_op jit(solution)/shard_map/all_gather | solution.py:256
  85.8 60.2 %all-to-all-start = ((bf16[4,64,2048]{2,1,0:T(8,128)(2,1)}), bf16[4,64,2048]{2,1,0:T(8,128)(2,1)S(1)}, u32[]{:S(2)}, u32[]{:S(2)}) async-start(bf16[4,64,2048]{2,1,0:T(8,128)(2,1)} %pad_maximum_fusion.9), calls=%async_computation | async-start | bytes 2097152 | tf_op jit(solution)/shard_map/all_to_all | solution.py:226
  101.8 49.5 %collective-permute-start.23 = (bf16[2,64,2048]{2,1,0:T(8,128)(2,1)}, bf16[2,64,2048]{2,1,0:T(8,128)(2,1)}, u32[]{:S(2)}, u32[]{:S(2)}) collective-permute-start(bf16[2,64,2048]{2,1,0:T(8,128)(2,1)} %dynamic-slice_bitcast_fusion.17), channel_id=1, source_target_pairs={{0,16},{16,0},{1,17},{17,1},{2,18},{18,2},{3,19},{19,3},{4,20},{20... | collective-permute-start | bytes 1572872 | tf_op jit(solution)/shard_map/ppermute | solution.py:183
  156.3 91.2 %all-to-all-start.2 = ((bf16[4,64,2048]{2,1,0:T(8,128)(2,1)}), bf16[4,64,2048]{2,1,0:T(8,128)(2,1)}, u32[]{:S(2)}, u32[]{:S(2)}) async-start(bf16[4,64,2048]{2,1,0:T(8,128)(2,1)} %pad_maximum_fusion.12), calls=%async_computation.2 | async-start | bytes 2097152 | tf_op jit(solution)/shard_map/all_to_all | solution.py:226
  160.6 266.1 %all-gather.19.cloned.1.call-start = ((), (), s32[]{:S(2)}) async-start(), calls=%async_computation.15 | async-start | bytes 4718592 | tf_op jit(solution)/shard_map/all_gather | solution.py:256
  244.4 48.9 %collective-permute-start.8 = (bf16[4,64,2048]{2,1,0:T(8,128)(2,1)}, bf16[4,64,2048]{2,1,0:T(8,128)(2,1)}, u32[]{:S(2)}, u32[]{:S(2)}) collective-permute-start(bf16[4,64,2048]{2,1,0:T(8,128)(2,1)} %get-tuple-element.70), channel_id=1, source_target_pairs={{0,16},{1,17},{16,0},{17,1},{2,18},{3,19},{18,2},{19,3},{4,20},{5,... | collective-permute-start | bytes 3145736 | tf_op jit(solution)/shard_map/ppermute | solution.py:183
  244.7 48.6 %collective-permute-start.9 = (bf16[4,64,2048]{2,1,0:T(8,128)(2,1)}, bf16[4,64,2048]{2,1,0:T(8,128)(2,1)}, u32[]{:S(2)}, u32[]{:S(2)}) collective-permute-start(bf16[4,64,2048]{2,1,0:T(8,128)(2,1)} %get-tuple-element.69), channel_id=1, source_target_pairs={{0,17},{1,16},{16,1},{17,0},{2,19},{3,18},{18,3},{19,2},{4,21},{5,... | collective-permute-start | bytes 3145736 | tf_op jit(solution)/shard_map/ppermute | solution.py:183
  247.5 698.2 %reduce-scatter.9.cloned.1.call-start = ((), (), s32[]{:S(2)}) async-start(), calls=%async_computation.17 | async-start | bytes 1310720 | tf_op jit(solution)/shard_map/reduce_scatter | solution.py:269
  247.5 66.9 %collective-permute-start.24 = (bf16[4,64,2048]{2,1,0:T(8,128)(2,1)}, bf16[4,64,2048]{2,1,0:T(8,128)(2,1)S(1)}, u32[]{:S(2)}, u32[]{:S(2)}) collective-permute-start(bf16[4,64,2048]{2,1,0:T(8,128)(2,1)} %all-to-all-done.2), channel_id=1, source_target_pairs={{0,1},{1,0},{16,17},{17,16},{2,3},{3,2},{18,19},{19,18},{4,5},{5,4... | collective-permute-start | bytes 3145736 | tf_op jit(solution)/shard_map/ppermute | solution.py:183
  248.9 87.8 %collective-permute-start.25 = (bf16[4,64,2048]{2,1,0:T(8,128)(2,1)}, bf16[4,64,2048]{2,1,0:T(8,128)(2,1)S(1)}, u32[]{:S(2)}, u32[]{:S(2)}) collective-permute-start(bf16[4,64,2048]{2,1,0:T(8,128)(2,1)} %all-to-all-done.2), channel_id=1, source_target_pairs={{0,16},{1,17},{16,0},{17,1},{2,18},{3,19},{18,2},{19,3},{4,20},{5,... | collective-permute-start | bytes 3145736 | tf_op jit(solution)/shard_map/ppermute | solution.py:183
  269.5 68.3 %collective-permute-start.26 = (bf16[4,64,2048]{2,1,0:T(8,128)(2,1)}, bf16[4,64,2048]{2,1,0:T(8,128)(2,1)S(1)}, u32[]{:S(2)}, u32[]{:S(2)}) collective-permute-start(bf16[4,64,2048]{2,1,0:T(8,128)(2,1)} %all-to-all-done.2), channel_id=1, source_target_pairs={{0,17},{1,16},{16,1},{17,0},{2,19},{3,18},{18,3},{19,2},{4,21},{5,... | collective-permute-start | bytes 3145736 | tf_op jit(solution)/shard_map/ppermute | solution.py:183
  300.2 59.2 %collective-permute-start.10 = (bf16[4,64,2048]{2,1,0:T(8,128)(2,1)S(1)}, bf16[4,64,2048]{2,1,0:T(8,128)(2,1)S(1)}, u32[]{:S(2)}, u32[]{:S(2)}) collective-permute-start(bf16[4,64,2048]{2,1,0:T(8,128)(2,1)S(1)} %get-tuple-element.46), channel_id=1, source_target_pairs={{0,1},{1,0},{16,17},{17,16},{2,3},{3,2},{18,19},{19,18},{4,5},{5,4... | collective-permute-start | bytes 3145736 | tf_op jit(solution)/shard_map/ppermute | solution.py:183
  315.5 65.1 %collective-permute-start.11 = (bf16[4,64,2048]{2,1,0:T(8,128)(2,1)S(1)}, bf16[4,64,2048]{2,1,0:T(8,128)(2,1)S(1)}, u32[]{:S(2)}, u32[]{:S(2)}) collective-permute-start(bf16[4,64,2048]{2,1,0:T(8,128)(2,1)S(1)} %get-tuple-element.46), channel_id=1, source_target_pairs={{0,16},{1,17},{16,0},{17,1},{2,18},{3,19},{18,2},{19,3},{4,20},{5,... | collective-permute-start | bytes 3145736 | tf_op jit(solution)/shard_map/ppermute | solution.py:183
  584.5 417.1 %reduce-scatter.15.cloned.1.call-start = ((), (), s32[]{:S(2)}) async-start(), calls=%async_computation.20 | async-start | bytes 2621440 | tf_op jit(solution)/shard_map/reduce_scatter | solution.py:269
  591.6 411.9 %reduce-scatter.17.cloned.1.call-start = ((), (), s32[]{:S(2)}) async-start(), calls=%async_computation.21 | async-start | bytes 2621440 | tf_op jit(solution)/shard_map/reduce_scatter | solution.py:269
  605.5 411.3 %reduce-scatter.7.cloned.1.call-start = ((), (), s32[]{:S(2)}) async-start(), calls=%async_computation.16 | async-start | bytes 3932160 | tf_op jit(solution)/shard_map/reduce_scatter | solution.py:269
  662.0 366.2 %reduce-scatter.11.cloned.1.call-start = ((), (), s32[]{:S(2)}) async-start(), calls=%async_computation.18 | async-start | bytes 5242880 | tf_op jit(solution)/shard_map/reduce_scatter | solution.py:269
  694.9 116.8 %collective-permute-start.45 = (bf16[1024,2048]{1,0:T(8,128)(2,1)}, bf16[1024,2048]{1,0:T(8,128)(2,1)}, u32[]{:S(2)}, u32[]{:S(2)}) collective-permute-start(bf16[1024,2048]{1,0:T(8,128)(2,1)} %convolution_convert_fusion.3), channel_id=1, source_target_pairs={{0,8},{8,0},{1,9},{9,1},{2,10},{10,2},{3,11},{11,3},{4,12},{12,4},... | collective-permute-start | bytes 12582920 | tf_op jit(solution)/shard_map/ppermute | solution.py:183
  711.3 49.4 %collective-permute-start.35 = (bf16[4,64,2048]{2,1,0:T(8,128)(2,1)S(1)}, bf16[4,64,2048]{2,1,0:T(8,128)(2,1)S(1)}, u32[]{:S(2)}, u32[]{:S(2)}) collective-permute-start(bf16[4,64,2048]{2,1,0:T(8,128)(2,1)S(1)} %get-tuple-element.60), channel_id=1, source_target_pairs={{0,17},{1,16},{16,1},{17,0},{2,19},{3,18},{18,3},{19,2},{4,21},{5,... | collective-permute-start | bytes 3145736 | tf_op jit(solution)/shard_map/ppermute | solution.py:183
  722.1 60.1 %collective-permute-start.17 = (bf16[4,64,2048]{2,1,0:T(8,128)(2,1)S(1)}, bf16[4,64,2048]{2,1,0:T(8,128)(2,1)S(1)}, u32[]{:S(2)}, u32[]{:S(2)}) collective-permute-start(bf16[4,64,2048]{2,1,0:T(8,128)(2,1)S(1)} %get-tuple-element.65), channel_id=1, source_target_pairs={{0,1},{1,0},{16,17},{17,16},{2,3},{3,2},{18,19},{19,18},{4,5},{5,4... | collective-permute-start | bytes 3145736 | tf_op jit(solution)/shard_map/ppermute | solution.py:183
  737.2 66.7 %collective-permute-start.18 = (bf16[4,64,2048]{2,1,0:T(8,128)(2,1)S(1)}, bf16[4,64,2048]{2,1,0:T(8,128)(2,1)S(1)}, u32[]{:S(2)}, u32[]{:S(2)}) collective-permute-start(bf16[4,64,2048]{2,1,0:T(8,128)(2,1)S(1)} %get-tuple-element.67), channel_id=1, source_target_pairs={{0,16},{1,17},{16,0},{17,1},{2,18},{3,19},{18,2},{19,3},{4,20},{5,... | collective-permute-start | bytes 3145736 | tf_op jit(solution)/shard_map/ppermute | solution.py:183
  808.1 52.8 %all-to-all-start.3 = ((bf16[4,64,2048]{2,1,0:T(8,128)(2,1)}), bf16[4,64,2048]{2,1,0:T(8,128)(2,1)S(1)}, u32[]{:S(2)}, u32[]{:S(2)}) async-start(bf16[4,64,2048]{2,1,0:T(8,128)(2,1)} %get-tuple-element.83), calls=%async_computation.3 | async-start | bytes 2097152 | tf_op jit(solution)/shard_map/all_to_all | solution.py:229
  811.6 220.9 %reduce-scatter.13.cloned.1.call-start = ((), (), s32[]{:S(2)}) async-start(), calls=%async_computation.19 | async-start | bytes 5242880 | tf_op jit(solution)/shard_map/reduce_scatter | solution.py:269
  860.9 79.9 %all-to-all-start.1 = ((bf16[4,64,2048]{2,1,0:T(8,128)(2,1)}), bf16[4,64,2048]{2,1,0:T(8,128)(2,1)S(1)}, u32[]{:S(2)}, u32[]{:S(2)}) async-start(bf16[4,64,2048]{2,1,0:T(8,128)(2,1)} %get-tuple-element.84), calls=%async_computation.1 | async-start | bytes 2097152 | tf_op jit(solution)/shard_map/all_to_all | solution.py:229
  865.7 81.2 %collective-permute-start.36 = (bf16[2,64,2048]{2,1,0:T(8,128)(2,1)}, bf16[2,64,2048]{2,1,0:T(8,128)(2,1)S(1)}, u32[]{:S(2)}, u32[]{:S(2)}) collective-permute-start(bf16[2,64,2048]{2,1,0:T(8,128)(2,1)} %get-tuple-element.97), channel_id=1, source_target_pairs={{0,17},{1,16},{16,1},{17,0},{2,19},{3,18},{18,3},{19,2},{4,21},{5,... | collective-permute-start | bytes 1572872 | tf_op jit(solution)/shard_map/ppermute | solution.py:183
  867.7 79.3 %collective-permute-start.37 = (bf16[2,64,2048]{2,1,0:T(8,128)(2,1)}, bf16[2,64,2048]{2,1,0:T(8,128)(2,1)S(1)}, u32[]{:S(2)}, u32[]{:S(2)}) collective-permute-start(bf16[2,64,2048]{2,1,0:T(8,128)(2,1)} %get-tuple-element.96), channel_id=1, source_target_pairs={{0,16},{1,17},{16,0},{17,1},{2,18},{3,19},{18,2},{19,3},{4,20},{5,... | collective-permute-start | bytes 1572872 | tf_op jit(solution)/shard_map/ppermute | solution.py:183
  868.5 80.5 %collective-permute-start.38 = (bf16[2,64,2048]{2,1,0:T(8,128)(2,1)}, bf16[2,64,2048]{2,1,0:T(8,128)(2,1)}, u32[]{:S(2)}, u32[]{:S(2)}) collective-permute-start(bf16[2,64,2048]{2,1,0:T(8,128)(2,1)} %get-tuple-element.95), channel_id=1, source_target_pairs={{0,1},{1,0},{16,17},{17,16},{2,3},{3,2},{18,19},{19,18},{4,5},{5,4... | collective-permute-start | bytes 1572872 | tf_op jit(solution)/shard_map/ppermute | solution.py:183
  947.0 56.4 %collective-permute-start.42 = (bf16[128,512]{0,1:T(8,128)(2,1)S(1)}, bf16[128,512]{0,1:T(8,128)(2,1)S(1)}, u32[]{:S(2)}, u32[]{:S(2)}) collective-permute-start(bf16[128,512]{0,1:T(8,128)(2,1)S(1)} %bitcast.365), channel_id=1, source_target_pairs={{0,16},{16,0},{1,17},{17,1},{2,18},{18,2},{3,19},{19,3},{4,20},{20... | collective-permute-start | bytes 393224 | tf_op jit(solution)/shard_map/ppermute | solution.py:183
  (83 other events, 1576.7 us)
Sparse Core Ops, SparseCore 0:
  22.8 66.2 all-gather.8
  91.3 37.5 all-gather.10
  130.5 103.2 all-gather.12
  235.9 46.1 all-gather.14
  283.6 80.2 all-gather.16
  365.9 46.3 all-gather.18
  584.6 23.2 reduce-scatter.8
  610.3 42.5 reduce-scatter.14
  655.1 43.1 reduce-scatter.16
  700.6 59.5 reduce-scatter.6
  762.6 93.2 reduce-scatter.10
  858.1 95.2 reduce-scatter.12

commit v2 on v1

--- a/solution.py
+++ b/solution.py
@@ -16,6 +16,10 @@
 MASKED = -1e30
 Q_BLOCK = 256
 MLP_CHUNKS = 2
+TILE = 256
+VMEM = 56 * 2**20
+COST = pl.CostEstimate(flops=10**12, bytes_accessed=10**6, transcendentals=0)
+SHORT = pl.CostEstimate(flops=10**10, bytes_accessed=10**6, transcendentals=0)
 BF16 = jnp.bfloat16
 F32 = jnp.float32
 
@@ -155,7 +159,8 @@
             jax.ShapeDtypeStruct((length, pairs * PAIR), F32),
         ],
         scratch_shapes=[pltpu.VMEM((2, length, PAIR), BF16)] * 2,
-        compiler_params=pltpu.CompilerParams(vmem_limit_bytes=48 * 2**20),
+        compiler_params=pltpu.CompilerParams(vmem_limit_bytes=VMEM),
+        cost_estimate=COST,
         name="attention_forward",
     )(qkv, qkv, qkv, cosine, sine, starts)
 
@@ -174,13 +179,209 @@
         out_shape=jax.ShapeDtypeStruct((length, 3 * pairs * PAIR), BF16),
         scratch_shapes=[pltpu.VMEM((2, length, PAIR), BF16)] * 4
         + [pltpu.VMEM((length, PAIR), F32)] * 3,
-        compiler_params=pltpu.CompilerParams(vmem_limit_bytes=48 * 2**20),
+        compiler_params=pltpu.CompilerParams(vmem_limit_bytes=VMEM),
+        cost_estimate=SHORT,
         name="attention_backward",
     )(qkv, qkv, qkv, grads, logs, cosine, sine, starts)
 
 
+def add_terms(terms):
+    first_half = 2 * pl.program_id(0) < pl.num_programs(0)
+    total = None
+    for term in terms:
+        if isinstance(term, tuple):
+            value = jnp.where(first_half, term[0][...].astype(F32), term[1][...].astype(F32))
+        else:
+            value = term[...].astype(F32)
+        total = value if total is None else total + value
+    return total
+
+
+def take_terms(refs, kinds):
+    refs, terms = list(refs), []
+    for kind in kinds:
+        terms.append(refs.pop(0) if kind == 1 else (refs.pop(0), refs.pop(0)))
+    return terms, refs
+
+
+def store(out, values, order):
+    step = values.shape[1] // len(order or (0,))
+    for place, source in enumerate(order or (0,)):
+        out[:, place * step : (place + 1) * step] = values[
+            :, source * step : (source + 1) * step
+        ].astype(out.dtype)
+
+
+def add_rows(kinds, order, *refs):
+    terms, (out,) = take_terms(refs, kinds)
+    store(out, add_terms(terms), order)
+
+
+def norm_forward(kinds, order, *refs):
+    terms, (gain_ref, kept_ref, normed_ref) = take_terms(refs, kinds)
+    store(kept_ref, add_terms(terms), order)
+    normed_ref[...] = rms_scale(kept_ref[...].astype(F32), gain_ref[...]).astype(BF16)
+
+
+def norm_backward(kinds, order, *refs):
+    terms, (values_ref, gain_ref, above_ref, gain_grad_ref, *outs) = take_terms(refs, kinds)
+    grad = add_terms(terms)
+    values = values_ref[...].astype(F32)
+    scale = lax.rsqrt(jnp.mean(values * values, axis=-1, keepdims=True) + NORM_EPS)
+    scaled = values * scale
+    term = grad * gain_ref[...]
+    mean = jnp.mean(scaled * term, axis=-1, keepdims=True)
+    total = above_ref[...].astype(F32) + scale * (term - scaled * mean)
+
+    @pl.when(pl.program_id(0) == 0)
+    def _():
+        gain_grad_ref[...] = jnp.zeros_like(gain_grad_ref)
+
+    gain_grad_ref[...] += jnp.sum(grad * scaled, axis=0, keepdims=True)
+    for out in outs:
+        store(out, total, order)
+
+
+def feed_forward(normed_ref, above_ref, gate_up_ref, down_ref, hidden_ref, grad_ref):
+    length, tile = hidden_ref.shape
+    for row in range(0, length, Q_BLOCK):
+        at = slice(row, min(row + Q_BLOCK, length))
+        normed = normed_ref[at]
+        gate = dot(normed, gate_up_ref[:, :tile], ((1,), (0,)))
+        up = dot(normed, gate_up_ref[:, tile:], ((1,), (0,)))
+        hidden_grad = dot(above_ref[at], down_ref[...], ((1,), (0,)))
+        sigmoid = 1.0 / (1.0 + jnp.exp(-gate))
+        silu = gate * sigmoid
+        hidden_ref[at] = (silu * up).astype(BF16)
+        grad_ref[at, :tile] = (hidden_grad * up * (sigmoid + silu * (1.0 - sigmoid))).astype(BF16)
+        grad_ref[at, tile:] = (hidden_grad * silu).astype(BF16)
+
+
+def row_terms_specs(terms, width):
+    whole = [t for t in terms if not isinstance(t, tuple)][0]
+    rows = whole.size // width
+    block = min(rows // 2, 64)
+    steps = rows // block
+    row = pl.BlockSpec((block, width), lambda i: (i, 0))
+    first = pl.BlockSpec((block, width), lambda i: (jnp.minimum(i, steps // 2 - 1), 0))
+    second = pl.BlockSpec((block, width), lambda i: (jnp.maximum(i - steps // 2, 0), 0))
+    flat, kinds, specs = [], [], []
+    for term in terms:
+        parts = term if isinstance(term, tuple) else (term,)
+        flat += [part.reshape(-1, width) for part in parts]
+        specs += [first, second] if len(parts) == 2 else [row]
+        kinds.append(len(parts))
+    return rows, steps, row, flat, tuple(kinds), specs
+
+
+def run_add_rows(terms, order):
+    shape = terms[0].shape
+    width = shape[-1]
+    rows, steps, row, flat, kinds, specs = row_terms_specs(terms, width)
+    out = pl.pallas_call(
+        functools.partial(add_rows, kinds, order),
+        grid=(steps,),
+        in_specs=specs,
+        out_specs=row,
+        out_shape=jax.ShapeDtypeStruct((rows, width), BF16),
+        compiler_params=pltpu.CompilerParams(vmem_limit_bytes=VMEM),
+        name="add_rows",
+    )(*flat)
+    return out.reshape(shape)
+
+
+def run_norm_forward(terms, gain, kept, order=None):
+    shape = terms[0].shape
+    width = shape[-1]
+    rows, steps, row, flat, kinds, specs = row_terms_specs(terms, width)
+    whole = pl.BlockSpec((1, width), lambda i: (0, 0))
+    outs = pl.pallas_call(
+        functools.partial(norm_forward, kinds, order),
+        grid=(steps,),
+        in_specs=specs + [whole],
+        out_specs=[row, row],
+        out_shape=[jax.ShapeDtypeStruct((rows, width), kind) for kind in (kept, BF16)],
+        compiler_params=pltpu.CompilerParams(vmem_limit_bytes=VMEM),
+        cost_estimate=COST,
+        name="norm_forward",
+    )(*flat, gain[None])
+    return [out.reshape(shape) for out in outs]
+
+
+def run_norm_backward(terms, values, gain, above, types, cost, order=None):
+    shape = values.shape
+    width = shape[-1]
+    rows, steps, row, flat, kinds, specs = row_terms_specs(terms, width)
+    whole = pl.BlockSpec((1, width), lambda i: (0, 0))
+    grad, *outs = pl.pallas_call(
+        functools.partial(norm_backward, kinds, order),
+        grid=(steps,),
+        in_specs=specs + [row, whole, row],
+        out_specs=[whole] + [row] * len(types),
+        out_shape=[jax.ShapeDtypeStruct((1, width), F32)]
+        + [jax.ShapeDtypeStruct((rows, width), kind) for kind in types],
+        compiler_params=pltpu.CompilerParams(vmem_limit_bytes=VMEM),
+        cost_estimate=cost,
+        name="norm_backward",
+    )(*flat, values.reshape(rows, width), gain[None], above.reshape(rows, width))
+    return grad, [out.reshape(shape) for out in outs]
+
+
+def turned_product(left_ref, right_ref, out_ref):
+    out_ref[...] = dot(left_ref[...], right_ref[...], ((1,), (1,))).astype(BF16)
+
+
+def run_turned_product(left, right):
+    (length, depth), width = left.shape, right.shape[0]
+    tile = min(TILE, width)
+    return pl.pallas_call(
+        turned_product,
+        grid=(width // tile,),
+        in_specs=[
+            pl.BlockSpec((length, depth), lambda j: (0, 0)),
+            pl.BlockSpec((tile, depth), lambda j: (j, 0)),
+        ],
+        out_specs=pl.BlockSpec((length, tile), lambda j: (0, j)),
+        out_shape=jax.ShapeDtypeStruct((length, width), BF16),
+        compiler_params=pltpu.CompilerParams(vmem_limit_bytes=VMEM),
+        cost_estimate=COST,
+        name="turned_product",
+    )(left, right)
+
+
+def run_feed_forward(normed, above, weight, part_cols):
+    length, width = normed.shape
+    tile = min(TILE, part_cols)
+    whole = pl.BlockSpec((length, width), lambda j: (0, 0))
+    return pl.pallas_call(
+        feed_forward,
+        grid=(part_cols // tile,),
+        in_specs=[
+            whole,
+            whole,
+            pl.BlockSpec((width, 2 * tile), lambda j: (0, j)),
+            pl.BlockSpec((width, tile), lambda j: (0, 2 * part_cols // tile + j)),
+        ],
+        out_specs=[
+            pl.BlockSpec((length, tile), lambda j: (0, j)),
+            pl.BlockSpec((length, 2 * tile), lambda j: (0, j)),
+        ],
+        out_shape=[
+            jax.ShapeDtypeStruct((length, part_cols), BF16),
+            jax.ShapeDtypeStruct((length, 2 * part_cols), BF16),
+        ],
+        compiler_params=pltpu.CompilerParams(vmem_limit_bytes=VMEM),
+        cost_estimate=COST,
+        name="feed_forward",
+    )(normed, above, weight, weight)
+
+
 def swap(values, axis, size, step):
     return lax.ppermute(values, axis, [(i, i ^ step) for i in range(size)])
+
+
+def after(values, *others):
+    return lax.optimization_barrier((values,) + others)[0]
 
 
 def by_index(parts, index):
@@ -205,90 +406,143 @@
     length = segments.shape[1]
     piece_rows = chunk // nq
     rows = w_query.shape[0]
+    half = width // 2
 
     def pick(array, index, axis):
         return lax.dynamic_index_in_dim(array, index, axis, keepdims=False)
 
-    def permuted(values):
-        lead = values.shape[:-1]
-        return values.reshape(lead + (ny, 2 * nc, rows)).swapaxes(-3, -2).reshape(lead + (width,))
-
-    def unpermuted(values):
-        lead = values.shape[:-1]
-        return values.reshape(lead + (2 * nc, ny, rows)).swapaxes(-3, -2).reshape(lead + (width,))
-
-    def pieces_in(values):
-        values = permuted(values).reshape(batch, nq, piece_rows, width)
-        parts = [pick(values, quarter, 1)]
+    inward = tuple(y * 2 * nc + k for k in range(2 * nc) for y in range(ny))
+    outward = tuple(k * ny + y for y in range(ny) for k in range(2 * nc))
+
+    def over_y(blocks):
+        parts = [blocks(yi)]
         for step in range(1, ny):
-            parts.append(swap(pick(values, (yi ^ step) * nx + xi, 1), "y", ny, step))
-        ordered = jnp.concatenate(by_index(parts, yi), axis=0)
-        return lax.all_to_all(ordered, "ctx", 0, 0, tiled=True)
-
-    def pieces_out(piece):
-        held = lax.all_to_all(piece, "ctx", 0, 0, tiled=True)
+            parts.append(swap(blocks(yi ^ step), "y", ny, step))
+        return by_index(parts, yi)
+
+    def rows_for(values):
+        values = values.reshape(batch, nq, piece_rows, width)
+        return jnp.concatenate(over_y(lambda index: pick(values, index * nx + xi, 1)), axis=0)
+
+    def turn(pieces):
+        return lax.all_to_all(pieces, "ctx", 0, 0, tiled=True)
+
+    def pieces_out(held):
         held = held.reshape(ny, batch, piece_rows, width)
         parts = [pick(held, yi, 0)]
         for step in range(1, nq):
             parts.append(swap(pick(held, (quarter ^ step) // nx, 0), group, nq, step))
         ordered = jnp.stack(by_index(parts, quarter), axis=1)
-        return unpermuted(ordered.reshape(batch, chunk, width))
+        return ordered.reshape(batch, chunk, width)
+
+    corner = nq == 4 and nx == 2 and nc % 2 == 0
+    cut = nc // 2
 
     def gather_rows(piece):
         out = jnp.zeros((nc, nq, piece_rows, width), piece.dtype)
-        for step in range(nq):
-            part = piece if step == 0 else swap(piece, group, nq, step)
-            out = lax.dynamic_update_slice(out, part[:, None], (0, quarter ^ step, 0, 0))
-        return out.reshape(length, width)
-
-    def sum_rows(partial):
+
+        def put(out, part, step, start=0):
+            return lax.dynamic_update_slice(out, part[:, None], (start, quarter ^ step, 0, 0))
+
+        if not corner:
+            for step in range(nq):
+                out = put(out, piece if step == 0 else swap(piece, group, nq, step), step)
+            return out.reshape(length, width)
+        by_x, by_y = swap(piece, group, nq, 1), swap(piece, group, nq, 2)
+        far_x, far_y = swap(by_y[:cut], group, nq, 1), swap(by_x[cut:], group, nq, 2)
+        out = put(put(put(out, piece, 0), by_x, 1), by_y, 2)
+        return put(put(out, far_x, 3), far_y, 3, cut).reshape(length, width)
+
+    def row_terms(partial, *beside):
         partial = partial.reshape(nc, nq, piece_rows, width)
-        total = pick(partial, quarter, 1).astype(F32)
-        for step in range(1, nq):
-            total = total + swap(pick(partial, quarter ^ step, 1), group, nq, step).astype(F32)
-        return total
-
-    def fetch(blocks):
-        parts = [blocks(yi)]
-        for step in range(1, ny):
-            parts.append(swap(blocks(yi ^ step), "y", ny, step))
-        held = jnp.concatenate(by_index(parts, yi), axis=0)
+
+        def term(step):
+            return pick(partial, quarter ^ step, 1)
+
+        if not corner:
+            return [term(0)] + [swap(term(step), group, nq, step) for step in range(1, nq)]
+        far, to_x, to_y = term(3), term(1), term(2)
+        from_x, from_y = swap(far[:cut], group, nq, 1), swap(far[cut:], group, nq, 2)
+        x_first, y_last = swap(to_x[:cut], group, nq, 1), swap(to_y[cut:], group, nq, 2)
+        to_x, to_y = after(to_x[cut:], *beside), after(to_y[:cut], *beside)
+        to_x = (to_x.astype(F32) + from_y.astype(F32)).astype(BF16)
+        to_y = (to_y.astype(F32) + from_x.astype(F32)).astype(BF16)
+        return [
+            term(0),
+            (x_first, swap(to_x, group, nq, 1)),
+            (swap(to_y, group, nq, 2), y_last),
+        ]
+
+    def fetch(held):
         return lax.all_gather(held, ("core", "ctx"), axis=0, tiled=True)
 
     def columns(weight, index, start, count):
         share = weight.shape[1] // ny
         return lax.dynamic_slice_in_dim(weight, index * share + start, count, axis=1)
 
-    def settle(left, right):
-        half = width // 2
-        other = lax.dynamic_slice_in_dim(left, (1 - core) * half, half, axis=1)
-        mine = lax.dynamic_slice_in_dim(left, core * half, half, axis=1)
-        away = dot(other, right, ((0,), (0,))).astype(BF16)
-        came = swap(away, "core", 2, 1)
-        held = (dot(mine, right, ((0,), (0,))) + came.astype(F32)).astype(BF16)
-        return lax.psum_scatter(held, "ctx", scatter_dimension=0, tiled=True)
-
-    def own_rows(summed):
-        summed = summed.reshape(ny, rows, -1)
-        parts = [pick(summed, yi, 0)]
-        for step in range(1, ny):
-            parts.append(swap(pick(summed, yi ^ step, 0), "y", ny, step))
-        return by_index(parts, yi)
-
-    gains = lax.all_gather(
-        jnp.concatenate([attn_gain, mlp_gain])[None], ("core", "ctx", "y"), axis=0, tiled=True
-    )
+    def core_half(values, index):
+        return lax.dynamic_slice_in_dim(values, index * half, half, axis=1)
+
+    def partials(left, right, dim):
+        def term(index):
+            pair = (core_half(left, index), right) if dim == 0 else (left, core_half(right, index))
+            return dot(*pair, ((0,), (0,)))
+
+        came = swap(term(1 - core).astype(BF16), "core", 2, 1)
+        return (term(core) + came.astype(F32)).astype(BF16)
+
+    def settle(held, dim):
+        return lax.psum_scatter(held, "ctx", scatter_dimension=dim, tiled=True)
+
+    def own_rows(summed, dim):
+        return over_y(lambda index: lax.dynamic_slice_in_dim(summed, index * rows, rows, axis=dim))
+
+    def gain_settle(grads):
+        def add(values, axis, size):
+            return sum((swap(values, axis, size, step) for step in range(1, size)), values)
+
+        grads = add(add(add(grads, group, nq), "core", 2), "ctx", nc)
+        return pick(grads.reshape(2, 2 * nc * ny, rows), (core * nc + ctx) * ny + yi, 1)
+
+    head_cols = w_query.shape[1] // ny
+    hidden_cols = w_gate.shape[1] // ny
+    part_cols = hidden_cols // MLP_CHUNKS
+    out_turned, down_turned = w_out.T, w_down.T
+    wanted = [[(w, 0, head_cols) for w in (w_query, w_key, w_value, out_turned)]]
+    tile = min(TILE, part_cols)
+    tiles = part_cols // tile
+    for part in range(MLP_CHUNKS):
+        start = part * part_cols
+        wanted.append(
+            [(w, start + i * tile, tile) for i in range(tiles) for w in (w_gate, w_up)]
+            + [(down_turned, start, part_cols)]
+        )
+
+    def prepare(sources, *before):
+        def block(index):
+            return after(jnp.concatenate([columns(w, index, *p) for w, *p in sources], axis=1), *before)
+
+        return jnp.concatenate(over_y(block), axis=0)
+
+    x_rows = rows_for(tokens)
+    x_low = turn(x_rows)
+    held = prepare(wanted[0])
+    weights = [fetch(after(held, x_rows))]
+    for sources in wanted[1:]:
+        held = prepare(sources, held, x_rows)
+        weights.append(fetch(held))
+    qkv_weight, out_weight = weights[0][:, : 3 * head_cols], weights[0][:, 3 * head_cols :]
+
+    gains = jnp.concatenate([attn_gain, mlp_gain])[None]
+    for axis, size, index in (("y", ny, yi), ("ctx", nc, ctx), ("core", 2, core)):
+        step = 1
+        while step < size:
+            other = swap(gains, axis, size, step)
+            odd = (index & step) != 0
+            gains = jnp.concatenate([jnp.where(odd, other, gains), jnp.where(odd, gains, other)])
+            step *= 2
     gain_one = gains[:, :rows].reshape(width).astype(F32)
     gain_two = gains[:, rows:].reshape(width).astype(F32)
-
-    head_cols = w_query.shape[1] // ny
-    qkv_weight = fetch(
-        lambda index: jnp.concatenate(
-            [columns(w, index, 0, head_cols) for w in (w_query, w_key, w_value)], axis=1
-        )
-    )
-    out_turned = w_out.T
-    out_weight = fetch(lambda index: columns(out_turned, index, 0, head_cols))
 
     seg_parts = [segments] + [swap(segments, "y", ny, step) for step in range(1, ny)]
     all_segments = jnp.concatenate(by_index(seg_parts, yi), axis=0)
@@ -296,87 +550,94 @@
     cosine, sine = rope_tables(starts)
     starts = jnp.broadcast_to(starts[:, None], (length, PAIR))
 
-    x_piece = pieces_in(tokens).astype(F32)
-    normed = gather_rows(rms_scale(x_piece, gain_one).astype(BF16))
-    up_piece = pieces_in(cotangent)
-    upstream = gather_rows(up_piece)
-
-    hidden_cols = w_gate.shape[1] // ny
-    part_cols = hidden_cols // MLP_CHUNKS
-    down_turned = w_down.T
-    mlp_weights = []
-    for part in range(MLP_CHUNKS):
-        start = part * part_cols
-        gate_up = fetch(
-            lambda index: jnp.concatenate(
-                [columns(w, index, start, part_cols) for w in (w_gate, w_up)], axis=1
-            )
-        )
-        mlp_weights.append((gate_up, fetch(lambda index: columns(down_turned, index, start, part_cols))))
+    x_low, normed_piece = run_norm_forward([x_low], gain_one, BF16, inward)
+    normed = gather_rows(normed_piece)
+    up_piece = run_add_rows([turn(rows_for(after(cotangent, x_low)))], inward)
+    upstream = gather_rows(after(up_piece, normed))
 
     qkv = dot(normed, qkv_weight, ((1,), (0,)))
     attended, logs = run_attention_forward(qkv, cosine, sine, starts)
-    attn_sum = sum_rows(dot(attended, out_weight, ((1,), (1,))).astype(BF16))
-    residual = x_piece + attn_sum
-    normed_two = gather_rows(rms_scale(residual, gain_two).astype(BF16))
+    attn_terms = row_terms(dot(attended, out_weight, ((1,), (1,))).astype(BF16))
+    residual, normed_two = run_norm_forward([x_low] + attn_terms, gain_two, F32)
+    normed_two = gather_rows(normed_two)
 
     mlp_out = None
     back_two = None
-    mlp_grads = []
-    for gate_up, down in mlp_weights:
-        both = dot(normed_two, gate_up, ((1,), (0,)))
-        gate, up = both[:, :part_cols], both[:, part_cols:]
-        hidden_grad = dot(upstream, down, ((1,), (0,)))
-        sigmoid = jax.nn.sigmoid(gate)
-        silu = gate * sigmoid
-        hidden = (silu * up).astype(BF16)
-        gate_grad = hidden_grad * up * (sigmoid + silu * (1.0 - sigmoid))
-        both_grad = jnp.concatenate([gate_grad, hidden_grad * silu], axis=1).astype(BF16)
+    mlp_sums = []
+    wait_for = []
+    now_two = normed_two
+    for part in range(MLP_CHUNKS):
+        weight = weights[1 + part]
+        gate_up, down = weight[:, : 2 * part_cols], weight[:, 2 * part_cols :]
+        hidden, both_grad = run_feed_forward(now_two, upstream, weight, part_cols)
         term = dot(both_grad, gate_up, ((1,), (1,)))
         back_two = term if back_two is None else back_two + term
+        if part + 1 == MLP_CHUNKS:
+            back_two = back_two.astype(BF16)
+            hidden, both_grad = after(hidden, back_two), after(both_grad, back_two)
+        held_both, held_down = partials(normed_two, both_grad, 0), partials(hidden, upstream, 1)
+        sums = [(settle(held_down, 1), 1), (settle(held_both, 0), 0)]
+        if part + 1 < MLP_CHUNKS:
+            now_two = after(now_two, held_both, held_down)
+            wait_for += [summed for summed, _ in sums]
+        mlp_sums.append(sums)
         term = dot(hidden, down, ((1,), (1,)))
         mlp_out = term if mlp_out is None else mlp_out + term
-        mlp_grads.append((settle(normed_two, both_grad), settle(upstream, hidden)))
-
-    back_two = sum_rows(back_two.astype(BF16))
-    _, norm_two_back = jax.vjp(rms_scale, residual, gain_two)
-    residual_grad, gain_two_grad = norm_two_back(back_two)
-    residual_grad = residual_grad + up_piece.astype(F32)
-    residual_low = gather_rows(residual_grad.astype(BF16))
+
+    mlp_out = mlp_out.astype(BF16)
+    back_terms = row_terms(back_two, held_both, held_down, mlp_out)
+    back_terms[0] = after(back_terms[0], *wait_for)
+    gain_two_grad, (residual_grad, residual_low) = run_norm_backward(
+        back_terms, residual, gain_two, up_piece, [F32, BF16], COST
+    )
+    residual_low = gather_rows(residual_low)
     attended_grad = dot(residual_low, out_weight, ((1,), (0,))).astype(BF16)
-    out_grad = settle(residual_low, attended)
-
     qkv_grad = run_attention_backward(qkv, attended_grad, logs, cosine, sine, starts)
-    back_one = sum_rows(dot(qkv_grad, qkv_weight, ((1,), (1,))).astype(BF16))
-    qkv_weight_grad = settle(normed, qkv_grad)
-    _, norm_one_back = jax.vjp(rms_scale, x_piece, gain_one)
-    inputs_grad, gain_one_grad = norm_one_back(back_one)
-    grad_tokens = pieces_out((inputs_grad + residual_grad).astype(BF16)).astype(F32)
-    block_out = pieces_out((residual + sum_rows(mlp_out.astype(BF16))).astype(BF16))
-
-    gain_grads = lax.psum(
-        jnp.stack([gain_one_grad, gain_two_grad]), ("y", "core", "ctx", "tensor")
-    ).reshape(2, 2 * nc * ny, rows)
-    gain_grads = pick(gain_grads, (core * nc + ctx) * ny + yi, 1)
-
-    qkv_parts = own_rows(qkv_weight_grad)
+    attn_held = jnp.concatenate(
+        [partials(normed, qkv_grad, 0), partials(residual_low, after(attended, attended_grad), 0)], axis=1
+    )
+    attn_summed = settle(attn_held, 0)
+    back_one = run_turned_product(after(qkv_grad, attn_held, *[t for t, _ in mlp_sums[-1]]), weights[0])
+    one_terms = row_terms(back_one)
+    mlp_terms = row_terms(after(mlp_out, residual_low), attn_held)
+    block_out = turn(run_add_rows([after(residual, back_one)] + mlp_terms, outward))
+    gain_one_grad, (inputs_grad,) = run_norm_backward(
+        one_terms, x_low, gain_one, residual_grad, [BF16], SHORT, outward
+    )
+    block_out = pieces_out(after(block_out, inputs_grad))
+    grad_tokens = pieces_out(turn(inputs_grad)).astype(F32)
+    gain_grads = gain_settle(jnp.concatenate([gain_one_grad, gain_two_grad]))
+    mlp_grads = [
+        [
+            own_rows(after(summed, back_one if part + 1 < MLP_CHUNKS else inputs_grad), dim)
+            for summed, dim in pair
+        ]
+        for part, pair in enumerate(mlp_sums)
+    ]
+    attn_grads = own_rows(attn_summed, 0)
+
     grad_query, grad_key, grad_value = (
         jnp.concatenate(
-            [p[:, i * head_cols : (i + 1) * head_cols] for p in qkv_parts], axis=1
+            [p[:, i * head_cols : (i + 1) * head_cols] for p in attn_grads], axis=1
         ).astype(F32)
         for i in range(3)
     )
-    grad_out = jnp.concatenate(own_rows(out_grad), axis=1).T.astype(F32)
-    gate_up_parts = [own_rows(pair[0]) for pair in mlp_grads]
-    down_parts = [own_rows(pair[1]) for pair in mlp_grads]
+    grad_out = jnp.concatenate([p[:, 3 * head_cols :] for p in attn_grads], axis=1).T.astype(F32)
     grad_gate, grad_up = (
         jnp.concatenate(
-            [p[y][:, i * part_cols : (i + 1) * part_cols] for y in range(ny) for p in gate_up_parts],
+            [
+                pair[-1][y][:, (2 * j + i) * tile : (2 * j + i + 1) * tile]
+                for y in range(ny)
+                for pair in mlp_grads
+                for j in range(tiles)
+            ],
             axis=1,
         ).astype(F32)
         for i in range(2)
     )
-    grad_down = jnp.concatenate([p[y] for y in range(ny) for p in down_parts], axis=1).T.astype(F32)
+    grad_down = jnp.concatenate(
+        [pair[0][y] for y in range(ny) for pair in mlp_grads], axis=0
+    ).astype(F32)
     return (
         block_out,
         grad_tokens,

time: 1070 us -> 840 us (0.79)
  waiting for transfers between devices: 464 us -> 295 us
  blocking collectives: 111 us -> 0 us
  Pallas kernels: 53.3 us -> 136 us
  matrix products: 203 us -> 149 us
  starting transfers between devices: 68.7 us -> 101 us
  local copies, waits for them, and re-layouts: 103 us -> 90.4 us
    ppermute x51 -> x74, waiting for transfers between devices: 424 us -> 194 us  [swap(): return lax.ppermute(values, axis, [(i, i ^ step) for i in range(size)])]
    pallas_call x0 -> x9, Pallas kernels: none -> 80.3 us  [the longest x2 39.7 us: run_feed_forward(): pl.pallas_call(feed_forward, grid=(part_cols // tile,), in_specs=[whole,...]
    psum x1 -> x0, blocking collectives: 71 us -> none  [per_device(): lax.psum(jnp.stack([gain_one_grad, gain_two_grad]), ('y', 'core', 'ctx',...]
    dot_general x24 -> x19, matrix products: 203 us -> 149 us  [dot(): lax.dot_general(left, right, (contract, ((), ())), preferred_element_type...]
    all_gather x1 -> x0, blocking collectives: 40.4 us -> none  [per_device(): lax.all_gather(jnp.concatenate([attn_gain, mlp_gain])[None], ('core', 'ct...]
    all_to_all x4, waiting for transfers between devices: 39.1 us -> 74.8 us  [turn(): return lax.all_to_all(pieces, 'ctx', 0, 0, tiled=True)]
    ppermute x51 -> x74, starting transfers between devices: 52.5 us -> 82.1 us  [swap(): return lax.ppermute(values, axis, [(i, i ^ step) for i in range(size)])]
    reduce_scatter x6 -> x5, waiting for transfers between devices: 0.07 us -> 18 us  [settle(): return lax.psum_scatter(held, 'ctx', scatter_dimension=dim, tiled=True)]
  transfers between devices with their start and end apart: 67 -> 86, of which waited for: 35 -> 40; matrix products, arithmetic and copies ran while one was open for 27% -> 33% of each run, Pallas kernels for 5% -> 16%
where the time goes in v2:
time: 840 us; the launch traced here: 832 us
  waiting for transfers between devices  295 us (35%)
  matrix products  149 us (18%)
  Pallas kernels  136 us (16%)
  starting transfers between devices  101 us (12%)
  local copies, waits for them, and re-layouts  90.4 us (11%)
  other arithmetic  42.7 us (5%)
  between operations  16.3 us (2%)
    ppermute x74, waiting for transfers between devices, swap(): return lax.ppermute(values, axis, [(i, i ^ step) for i in range(size)])  194 us
    dot_general x19, matrix products, dot(): lax.dot_general(left, right, (contract, ((), ())), preferred_element_type...  149 us
    ppermute x74, starting transfers between devices, swap(): return lax.ppermute(values, axis, [(i, i ^ step) for i in range(size)])  82.1 us
    all_to_all x4, waiting for transfers between devices, turn(): return lax.all_to_all(pieces, 'ctx', 0, 0, tiled=True)  74.8 us
    pallas_call x2, Pallas kernels, run_feed_forward(): pl.pallas_call(feed_forward, grid=(part_cols // tile,), in_specs=[whole,...  39.7 us
    pallas_call x1, Pallas kernels, run_attention_backward(): pl.pallas_call(attention_backward, grid=(pairs, 3), in_specs=[column(0),...  36.3 us
    unnamed x115, local copies, waits for them, and re-layouts  26.8 us
    dynamic_update_slice x20, local copies, waits for them, and re-layouts, put(): lax.dynamic_update_slice(out, part[:, None], (start, quarter ^ step, 0, 0))  20.9 us
  transfers between devices with their start and end apart: 86, of which 40 were waited for; matrix products, arithmetic and copies ran while one was open for 33% of the time, Pallas kernels for 16%

profile of v2, /device:TPU:0, one launch (start us, length us, event | category | flops | bytes accessed | tf_op | source)
XLA Modules:
  0.0 831.7 jit_solution(14315297026273766914)
XLA Ops:
  14.9 9.2 %collective-permute-done = bf16[2,64,2048]{2,1,0:T(8,128)(2,1)S(1)} collective-permute-done((bf16[2,64,2048]{2,1,0:T(8,128)(2,1)S(1)}, bf16[2,64,2048]{2,1,0:T(8,128)(2,1)S(1)}, u32[]{:S(2)}, u32[]{:S(2)}) %collective-permute-start) | collective-permute-done | bytes 524320 | tf_op jit(solution)/shard_map/ppermute | solution.py:380
  26.3 8.2 collective-permute-done.9
  77.4 7.9 collective-permute-done.26
  87.5 41.7 %all-to-all-done = bf16[4,64,2048]{2,1,0:T(8,128)(2,1)S(1)} async-done(((bf16[4,64,2048]{2,1,0:T(8,128)(2,1)}), bf16[4,64,2048]{2,1,0:T(8,128)(2,1)S(1)}, u32[]{:S(2)}, u32[]{:S(2)}) %all-to-all-start) | async-done | bytes 1048608 | tf_op jit(solution)/shard_map/all_to_all | solution.py:428
  140.8 21.9 %all-to-all-done.1 = bf16[4,64,2048]{2,1,0:T(8,128)(2,1)} async-done(((bf16[4,64,2048]{2,1,0:T(8,128)(2,1)}), bf16[4,64,2048]{2,1,0:T(8,128)(2,1)}, u32[]{:S(2)}, u32[]{:S(2)}) %all-to-all-start.1) | async-done | bytes 1048608 | tf_op jit(solution)/shard_map/all_to_all | solution.py:428
  177.9 8.5 %collective-permute-done.7 = bf16[2,64,2048]{2,1,0:T(8,128)(2,1)S(1)} collective-permute-done((bf16[2,64,2048]{2,1,0:T(8,128)(2,1)S(1)}, bf16[2,64,2048]{2,1,0:T(8,128)(2,1)S(1)}, u32[]{:S(2)}, u32[]{:S(2)}) %collective-permute-start.7) | collective-permute-done | bytes 524320 | tf_op jit(solution)/shard_map/ppermute | solution.py:380
  191.0 12.0 %fusion.4.q_ref.k_ref.v_ref = f32[1024,1536]{1,0:T(8,128)} fusion(bf16[1024,2048]{1,0:T(8,128)(2,1)} %bitcast.15, bf16[2048,2048]{1,0:T(8,128)(2,1)} %all-gather.4.cloned.1.call-done.right_ref), kind=kOutput, calls=%fused_computation.8 | convolution fusion | flops 6442450944 | bytes 16777216 | tf_op jit(solution)/shard_map/dot_general | solution.py:48
  204.0 19.8 %attention_forward.1 = (bf16[1024,512]{1,0:T(8,128)(2,1)}, f32[1024,512]{1,0:T(8,128)}) custom-call(f32[1024,1536]{1,0:T(8,128)} %fusion.4.q_ref.k_ref.v_ref, f32[1024,1536]{1,0:T(8,128)} %fusion.4.q_ref.k_ref.v_ref, f32[1024,1536]{1,0:T(8,128)} %fusion.4.q_ref.k_ref.v_ref, f32[1024,128]{1,0:T(8,128)} %get-tuple-element.258.cos_ref, ...), custom_call_target="tpu_custom_call" | custom-call | flops 999999995904 | bytes 1000000 | tf_op jit(solution)/shard_map/attention_forward/pallas_call | solution.py:152
  246.1 16.2 %collective-permute-done.14 = bf16[2,64,2048]{2,1,0:T(8,128)(2,1)S(1)} collective-permute-done((bf16[2,64,2048]{2,1,0:T(8,128)(2,1)S(1)}, bf16[2,64,2048]{2,1,0:T(8,128)(2,1)S(1)}, u32[]{:S(2)}, u32[]{:S(2)}) %collective-permute-start.14) | collective-permute-done | bytes 524320 | tf_op jit(solution)/shard_map/ppermute | solution.py:380
  273.6 8.3 %collective-permute-done.13 = bf16[2,64,2048]{2,1,0:T(8,128)(2,1)S(1)} collective-permute-done((bf16[2,64,2048]{2,1,0:T(8,128)(2,1)S(1)}, bf16[2,64,2048]{2,1,0:T(8,128)(2,1)S(1)}, u32[]{:S(2)}, u32[]{:S(2)}) %collective-permute-start.13) | collective-permute-done | bytes 524320 | tf_op jit(solution)/shard_map/ppermute | solution.py:380
  297.3 13.2 %collective-permute-done.18 = bf16[4,64,2048]{2,1,0:T(8,128)(2,1)S(1)} collective-permute-done((bf16[4,64,2048]{2,1,0:T(8,128)(2,1)}, bf16[4,64,2048]{2,1,0:T(8,128)(2,1)S(1)}, u32[]{:S(2)}, u32[]{:S(2)}) %collective-permute-start.18) | collective-permute-done | bytes 1048608 | tf_op jit(solution)/shard_map/ppermute | solution.py:380
  324.6 20.2 %feed_forward.2 = (bf16[1024,1024]{1,0:T(8,128)(2,1)}, bf16[1024,2048]{1,0:T(8,128)(2,1)}) custom-call(bf16[1024,2048]{1,0:T(8,128)(2,1)} %bitcast.47.normed_ref, bf16[1024,2048]{1,0:T(8,128)(2,1)} %bitcast.62.above_ref, bf16[2048,3072]{1,0:T(8,128)(2,1)} %all-gather.6.cloned.1.call-done.gate_up_ref.down_ref, ...), custom_call_target="tpu_custom_call" | custom-call | flops 999999995904 | bytes 1000000 | tf_op jit(solution)/shard_map/feed_forward/pallas_call | solution.py:356
  350.9 7.9 convolution_convert_fusion.3
  366.5 10.8 %add_convert_fusion.3 = bf16[1024,2048]{1,0:T(8,128)(2,1)} fusion(bf16[1024,2048]{1,0:T(8,128)(2,1)} %collective-permute-done.27, bf16[1024,2048]{1,0:T(8,128)(2,1)} %get-tuple-element.58, bf16[1024,2048]{1,0:T(8,128)(2,1)} %bitcast.47.normed_ref, s32[]{:T(128)S(6)} %select_n.504), kind=kOutput, calls=%fused_computation.7 | convolution fusion | flops 4301258752 | bytes 14680068 | tf_op jit(solution)/shard_map/dot_general | solution.py:48
  377.6 8.0 all-gather.8.cloned.1.call-done.gate_up_ref.down_ref
  385.6 19.5 %feed_forward.3 = (bf16[1024,1024]{1,0:T(8,128)(2,1)}, bf16[1024,2048]{1,0:T(8,128)(2,1)}) custom-call(bf16[1024,2048]{1,0:T(8,128)(2,1)} %bitcast.47.normed_ref, bf16[1024,2048]{1,0:T(8,128)(2,1)} %bitcast.62.above_ref, bf16[2048,3072]{1,0:T(8,128)(2,1)} %all-gather.8.cloned.1.call-done.gate_up_ref.down_ref, ...), custom_call_target="tpu_custom_call" | custom-call | flops 999999995904 | bytes 1000000 | tf_op jit(solution)/shard_map/feed_forward/pallas_call | solution.py:356
  405.1 14.8 %fusion = f32[1024,2048]{1,0:T(8,128)} fusion(bf16[1024,2048]{1,0:T(8,128)(2,1)} %get-tuple-element.65, bf16[2048,3072]{1,0:T(8,128)(2,1)} %all-gather.8.cloned.1.call-done.gate_up_ref.down_ref), kind=kOutput, calls=%fused_computation | convolution fusion | flops 8589934592 | bytes 20971520 | tf_op jit(solution)/shard_map/dot_general | solution.py:48
  420.0 12.5 %add_convert_fusion.2 = bf16[1024,2048]{1,0:T(8,128)(2,1)S(1)} fusion(f32[1024,2048]{1,0:T(8,128)} %fusion, bf16[1024,2048]{1,0:T(8,128)(2,1)} %get-tuple-element.58, bf16[2048,3072]{1,0:T(8,128)(2,1)S(1)} %copy-done.24), kind=kOutput, calls=%fused_computation.6 | convolution fusion | flops 8594128896 | bytes 25165824 | tf_op jit(solution)/shard_map/dot_general | solution.py:48
  432.5 10.9 %convolution_convert_fusion.2 = bf16[1024,2048]{1,0:T(8,128)(2,1)} fusion(bf16[1024,2048]{1,0:T(8,128)(2,1)} %get-tuple-element.65, bf16[1024,2048]{1,0:T(8,128)(2,1)} %bitcast.47.normed_ref, s32[]{:T(128)S(6)} %select_n.505), kind=kOutput, calls=%fused_computation.20 | convolution fusion | flops 4297064448 | bytes 10485764 | tf_op jit(solution)/shard_map/dot_general | solution.py:48
  451.7 9.2 %fusion.8 = f32[1024,2048]{1,0:T(8,128)} fusion(bf16[1024,1024]{1,0:T(8,128)(2,1)S(1)} %copy-done.38, bf16[2048,3072]{1,0:T(8,128)(2,1)} %all-gather.8.cloned.1.call-done.gate_up_ref.down_ref), kind=kOutput, calls=%fused_computation.11 | convolution fusion | flops 4294967296 | bytes 14680064 | tf_op jit(solution)/shard_map/dot_general | solution.py:48
  461.0 9.7 %add_convert_fusion = bf16[1024,2048]{1,0:T(8,128)(2,1)} fusion(f32[1024,2048]{1,0:T(8,128)} %fusion.8, bf16[1024,1024]{1,0:T(8,128)(2,1)S(1)} %copy-done.37, bf16[2048,3072]{1,0:T(8,128)(2,1)} %all-gather.6.cloned.1.call-done.gate_up_ref.down_ref), kind=kOutput, calls=%fused_computation.4 | convolution fusion | flops 4299161600 | bytes 18874368 | tf_op jit(solution)/shard_map/dot_general | solution.py:48
  476.8 10.7 %add_convert_fusion.1 = bf16[1024,2048]{1,0:T(8,128)(2,1)} fusion(bf16[1024,2048]{1,0:T(8,128)(2,1)} %collective-permute-done.31, bf16[1024,2048]{1,0:T(8,128)(2,1)} %get-tuple-element.65, bf16[1024,2048]{1,0:T(8,128)(2,1)} %bitcast.47.normed_ref, s32[]{:T(128)S(6)} %select_n.504), kind=kOutput, calls=%fused_computation.5 | convolution fusion | flops 4301258752 | bytes 14680068 | tf_op jit(solution)/shard_map/dot_general | solution.py:48
  495.4 12.9 %reduce-scatter.8.cloned.1.call-done = bf16[256,2048]{1,0:T(8,128)(2,1)} async-done(((bf16[1024,2048]{1,0:T(8,128)(2,1)}), bf16[256,2048]{1,0:T(8,128)(2,1)}) %reduce-scatter.8.cloned.1.call-update) | async-done | bytes 1048592 | tf_op jit(solution)/shard_map/reduce_scatter | solution.py:495
  518.7 21.5 %collective-permute-done.39 = bf16[4,64,2048]{2,1,0:T(8,128)(2,1)S(1)} collective-permute-done((bf16[4,64,2048]{2,1,0:T(8,128)(2,1)}, bf16[4,64,2048]{2,1,0:T(8,128)(2,1)S(1)}, u32[]{:S(2)}, u32[]{:S(2)}) %collective-permute-start.39) | collective-permute-done | bytes 1048608 | tf_op jit(solution)/shard_map/ppermute | solution.py:380
  543.6 9.6 %collective-permute-done.40 = bf16[2,64,2048]{2,1,0:T(8,128)(2,1)S(1)} collective-permute-done((bf16[2,64,2048]{2,1,0:T(8,128)(2,1)S(1)}, bf16[2,64,2048]{2,1,0:T(8,128)(2,1)S(1)}, u32[]{:S(2)}, u32[]{:S(2)}) %collective-permute-start.40) | collective-permute-done | bytes 524320 | tf_op jit(solution)/shard_map/ppermute | solution.py:380
  561.0 36.3 %attention_backward.1.left_ref = bf16[1024,1536]{1,0:T(8,128)(2,1)} custom-call(f32[1024,1536]{1,0:T(8,128)} %fusion.4.q_ref.k_ref.v_ref, f32[1024,1536]{1,0:T(8,128)} %fusion.4.q_ref.k_ref.v_ref, f32[1024,1536]{1,0:T(8,128)} %fusion.4.q_ref.k_ref.v_ref, bf16[1024,512]{1,0:T(8,128)(2,1)} %fusion.34.do_ref, f32[1024,512]{1,0:T(8,128)} %get-tuple-element.71.lse_ref, ...), custom_call_target="tpu_custom_call" | custom-call | flops 10000000000 | bytes 1000000 | tf_op jit(solution)/shard_map/attention_backward/pallas_call | solution.py:172
  633.9 12.3 %turned_product.1 = bf16[1024,2048]{1,0:T(8,128)(2,1)} custom-call(bf16[1024,1536]{1,0:T(8,128)(2,1)} %attention_backward.1.left_ref, bf16[2048,2048]{1,0:T(8,128)(2,1)} %all-gather.4.cloned.1.call-done.right_ref), custom_call_target="tpu_custom_call" | custom-call | flops 999999995904 | bytes 1000000 | tf_op jit(solution)/shard_map/turned_product/pallas_call | solution.py:337
  700.5 10.1 %collective-permute-done.54 = bf16[2,64,2048]{2,1,0:T(8,128)(2,1)S(1)} collective-permute-done((bf16[2,64,2048]{2,1,0:T(8,128)(2,1)S(1)}, bf16[2,64,2048]{2,1,0:T(8,128)(2,1)S(1)}, u32[]{:S(2)}, u32[]{:S(2)}) %collective-permute-start.54) | collective-permute-done | bytes 524320 | tf_op jit(solution)/shard_map/ppermute | solution.py:380
  737.4 8.1 collective-permute-done.71
  768.2 11.3 %all-to-all-done.3 = bf16[4,64,2048]{2,1,0:T(8,128)(2,1)S(1)} async-done(((bf16[4,64,2048]{2,1,0:T(8,128)(2,1)}), bf16[4,64,2048]{2,1,0:T(8,128)(2,1)S(1)}, u32[]{:S(2)}, u32[]{:S(2)}) %all-to-all-start.3) | async-done | bytes 1048608 | tf_op jit(solution)/shard_map/all_to_all | solution.py:428
  795.7 10.2 %collective-permute-done.59 = bf16[2,64,2048]{2,1,0:T(8,128)(2,1)S(1)} collective-permute-done((bf16[2,64,2048]{2,1,0:T(8,128)(2,1)S(1)}, bf16[2,64,2048]{2,1,0:T(8,128)(2,1)S(1)}, u32[]{:S(2)}, u32[]{:S(2)}) %collective-permute-start.59) | collective-permute-done | bytes 524320 | tf_op jit(solution)/shard_map/ppermute | solution.py:380
  811.1 9.4 %collective-permute-done.69 = bf16[128,2048]{1,0:T(8,128)(2,1)S(1)} collective-permute-done((bf16[128,2048]{1,0:T(8,128)(2,1)S(1)}, bf16[128,2048]{1,0:T(8,128)(2,1)S(1)}, u32[]{:S(2)}, u32[]{:S(2)}) %collective-permute-start.69) | collective-permute-done | bytes 524320 | tf_op jit(solution)/shard_map/ppermute | solution.py:380
  (418 shorter events, 372.5 us)
Async XLA Ops:
  7.2 183.8 %all-gather.4.cloned.1.call-start = ((), (), s32[]{:S(2)}) async-start(), calls=%async_computation.9 | async-start | bytes 9437184 | tf_op jit(solution)/shard_map/all_gather | solution.py:477
  39.7 35.3 %collective-permute-start.21 = (bf16[2,64,2048]{2,1,0:T(8,128)(2,1)}, bf16[2,64,2048]{2,1,0:T(8,128)(2,1)}, u32[]{:S(2)}, u32[]{:S(2)}) collective-permute-start(bf16[2,64,2048]{2,1,0:T(8,128)(2,1)} %dynamic-slice_bitcast_fusion.31), channel_id=1, source_target_pairs={{0,16},{16,0},{1,17},{17,1},{2,18},{18,2},{3,19},{19,3},{4,20},{20... | collective-permute-start | bytes 1572872 | tf_op jit(solution)/shard_map/ppermute | solution.py:380
  69.2 59.9 %all-to-all-start = ((bf16[4,64,2048]{2,1,0:T(8,128)(2,1)}), bf16[4,64,2048]{2,1,0:T(8,128)(2,1)S(1)}, u32[]{:S(2)}, u32[]{:S(2)}) async-start(bf16[4,64,2048]{2,1,0:T(8,128)(2,1)} %pad_maximum_fusion.5), calls=%async_computation | async-start | bytes 2097152 | tf_op jit(solution)/shard_map/all_to_all | solution.py:428
  75.0 249.6 %all-gather.6.cloned.1.call-start = ((), (), s32[]{:S(2)}) async-start(), calls=%async_computation.10 | async-start | bytes 14155776 | tf_op jit(solution)/shard_map/all_gather | solution.py:477
  86.7 79.4 %collective-permute-start.29 = (bf16[128,3072]{1,0:T(8,128)(2,1)}, bf16[128,3072]{1,0:T(8,128)(2,1)}, u32[]{:S(2)}, u32[]{:S(2)}) collective-permute-start(bf16[128,3072]{1,0:T(8,128)(2,1)} %copy-done.22), channel_id=1, source_target_pairs={{0,16},{16,0},{1,17},{17,1},{2,18},{18,2},{3,19},{19,3},{4,20},{20... | collective-permute-start | bytes 2359304 | tf_op jit(solution)/shard_map/ppermute | solution.py:380
  129.2 33.5 %all-to-all-start.1 = ((bf16[4,64,2048]{2,1,0:T(8,128)(2,1)}), bf16[4,64,2048]{2,1,0:T(8,128)(2,1)}, u32[]{:S(2)}, u32[]{:S(2)}) async-start(bf16[4,64,2048]{2,1,0:T(8,128)(2,1)} %pad_maximum_fusion.7), calls=%async_computation.1 | async-start | bytes 2097152 | tf_op jit(solution)/shard_map/all_to_all | solution.py:428
  133.9 251.7 %all-gather.8.cloned.1.call-start = ((), (), s32[]{:S(2)}) async-start(), calls=%async_computation.11 | async-start | bytes 14155776 | tf_op jit(solution)/shard_map/all_gather | solution.py:477
  137.6 34.9 %collective-permute-start.6 = (bf16[4,64,2048]{2,1,0:T(8,128)(2,1)}, bf16[4,64,2048]{2,1,0:T(8,128)(2,1)S(1)}, u32[]{:S(2)}, u32[]{:S(2)}) collective-permute-start(bf16[4,64,2048]{2,1,0:T(8,128)(2,1)} %bitcast.373), channel_id=1, source_target_pairs={{0,16},{1,17},{16,0},{17,1},{2,18},{3,19},{18,2},{19,3},{4,20},{5,... | collective-permute-start | bytes 3145736 | tf_op jit(solution)/shard_map/ppermute | solution.py:380
  139.3 34.9 %collective-permute-start.5 = (bf16[4,64,2048]{2,1,0:T(8,128)(2,1)}, bf16[4,64,2048]{2,1,0:T(8,128)(2,1)S(1)}, u32[]{:S(2)}, u32[]{:S(2)}) collective-permute-start(bf16[4,64,2048]{2,1,0:T(8,128)(2,1)} %bitcast.374), channel_id=1, source_target_pairs={{0,1},{1,0},{16,17},{17,16},{2,3},{3,2},{18,19},{19,18},{4,5},{5,4... | collective-permute-start | bytes 3145736 | tf_op jit(solution)/shard_map/ppermute | solution.py:380
  168.9 326.4 %reduce-scatter.6.cloned.1.call-start = ((), (), s32[]{:S(2)}) async-start(), calls=%async_computation.12 | async-start | bytes 2621440 | tf_op jit(solution)/shard_map/reduce_scatter | solution.py:495
  188.5 45.6 %collective-permute-start.23 = (bf16[4,64,2048]{2,1,0:T(8,128)(2,1)}, bf16[4,64,2048]{2,1,0:T(8,128)(2,1)}, u32[]{:S(2)}, u32[]{:S(2)}) collective-permute-start(bf16[4,64,2048]{2,1,0:T(8,128)(2,1)} %bitcast.52), channel_id=1, source_target_pairs={{0,16},{1,17},{16,0},{17,1},{2,18},{3,19},{18,2},{19,3},{4,20},{5,... | collective-permute-start | bytes 3145736 | tf_op jit(solution)/shard_map/ppermute | solution.py:380
  190.0 48.1 %collective-permute-start.22 = (bf16[4,64,2048]{2,1,0:T(8,128)(2,1)}, bf16[4,64,2048]{2,1,0:T(8,128)(2,1)}, u32[]{:S(2)}, u32[]{:S(2)}) collective-permute-start(bf16[4,64,2048]{2,1,0:T(8,128)(2,1)} %bitcast.52), channel_id=1, source_target_pairs={{0,1},{1,0},{16,17},{17,16},{2,3},{3,2},{18,19},{19,18},{4,5},{5,4... | collective-permute-start | bytes 3145736 | tf_op jit(solution)/shard_map/ppermute | solution.py:380
  236.0 54.0 %collective-permute-start.24 = (bf16[2,64,2048]{2,1,0:T(8,128)(2,1)}, bf16[2,64,2048]{2,1,0:T(8,128)(2,1)}, u32[]{:S(2)}, u32[]{:S(2)}) collective-permute-start(bf16[2,64,2048]{2,1,0:T(8,128)(2,1)} %slice.459), channel_id=1, source_target_pairs={{0,1},{1,0},{16,17},{17,16},{2,3},{3,2},{18,19},{19,18},{4,5},{5,4... | collective-permute-start | bytes 1572872 | tf_op jit(solution)/shard_map/ppermute | solution.py:380
  243.8 29.7 %collective-permute-start.11 = (bf16[2,64,2048]{2,1,0:T(8,128)(2,1)S(1)}, bf16[2,64,2048]{2,1,0:T(8,128)(2,1)S(1)}, u32[]{:S(2)}, u32[]{:S(2)}) collective-permute-start(bf16[2,64,2048]{2,1,0:T(8,128)(2,1)S(1)} %get-tuple-element.132), channel_id=1, source_target_pairs={{0,1},{1,0},{16,17},{17,16},{2,3},{3,2},{18,19},{19,18},{4,5},{5,4... | collective-permute-start | bytes 1572872 | tf_op jit(solution)/shard_map/ppermute | solution.py:380
  245.0 36.9 %collective-permute-start.13 = (bf16[2,64,2048]{2,1,0:T(8,128)(2,1)S(1)}, bf16[2,64,2048]{2,1,0:T(8,128)(2,1)S(1)}, u32[]{:S(2)}, u32[]{:S(2)}) collective-permute-start(bf16[2,64,2048]{2,1,0:T(8,128)(2,1)S(1)} %add_convert_fusion.15), channel_id=1, source_target_pairs={{0,1},{1,0},{16,17},{17,16},{2,3},{3,2},{18,19},{19,18},{4,5},{5,4... | collective-permute-start | bytes 1572872 | tf_op jit(solution)/shard_map/ppermute | solution.py:380
  365.2 143.0 %reduce-scatter.8.cloned.1.call-start = ((), (), s32[]{:S(2)}) async-start(), calls=%async_computation.13 | async-start | bytes 5242880 | tf_op jit(solution)/shard_map/reduce_scatter | solution.py:495
  377.4 251.4 %reduce-scatter.10.cloned.1.call-start = ((), (), s32[]{:S(2)}) async-start(), calls=%async_computation.14 | async-start | bytes 2621440 | tf_op jit(solution)/shard_map/reduce_scatter | solution.py:495
  443.4 33.4 %collective-permute-start.31 = (bf16[1024,2048]{1,0:T(8,128)(2,1)}, bf16[1024,2048]{1,0:T(8,128)(2,1)}, u32[]{:S(2)}, u32[]{:S(2)}) collective-permute-start(bf16[1024,2048]{1,0:T(8,128)(2,1)} %convolution_convert_fusion.2), channel_id=1, source_target_pairs={{0,8},{8,0},{1,9},{9,1},{2,10},{10,2},{3,11},{11,3},{4,12},{12,4},... | collective-permute-start | bytes 12582920 | tf_op jit(solution)/shard_map/ppermute | solution.py:380
  444.1 64.2 %collective-permute-start.37 = (bf16[2,64,2048]{2,1,0:T(8,128)(2,1)S(1)}, bf16[2,64,2048]{2,1,0:T(8,128)(2,1)}, u32[]{:S(2)}, u32[]{:S(2)}) collective-permute-start(bf16[2,64,2048]{2,1,0:T(8,128)(2,1)S(1)} %get-tuple-element.123), channel_id=1, source_target_pairs={{0,16},{1,17},{16,0},{17,1},{2,18},{3,19},{18,2},{19,3},{4,20},{5,... | collective-permute-start | bytes 1572872 | tf_op jit(solution)/shard_map/ppermute | solution.py:380
  445.6 42.0 %collective-permute-start.33 = (bf16[2,64,2048]{2,1,0:T(8,128)(2,1)S(1)}, bf16[2,64,2048]{2,1,0:T(8,128)(2,1)}, u32[]{:S(2)}, u32[]{:S(2)}) collective-permute-start(bf16[2,64,2048]{2,1,0:T(8,128)(2,1)S(1)} %get-tuple-element.125), channel_id=1, source_target_pairs={{0,16},{1,17},{16,0},{17,1},{2,18},{3,19},{18,2},{19,3},{4,20},{5,... | collective-permute-start | bytes 1572872 | tf_op jit(solution)/shard_map/ppermute | solution.py:380
  446.1 62.1 %collective-permute-start.30 = (bf16[2,64,2048]{2,1,0:T(8,128)(2,1)S(1)}, bf16[2,64,2048]{2,1,0:T(8,128)(2,1)}, u32[]{:S(2)}, u32[]{:S(2)}) collective-permute-start(bf16[2,64,2048]{2,1,0:T(8,128)(2,1)S(1)} %get-tuple-element.126), channel_id=1, source_target_pairs={{0,1},{1,0},{16,17},{17,16},{2,3},{3,2},{18,19},{19,18},{4,5},{5,4... | collective-permute-start | bytes 1572872 | tf_op jit(solution)/shard_map/ppermute | solution.py:380
  495.3 138.6 %reduce-scatter.12.cloned.1.call-start = ((), (), s32[]{:S(2)}) async-start(), calls=%async_computation.15 | async-start | bytes 5242880 | tf_op jit(solution)/shard_map/reduce_scatter | solution.py:495
  518.0 288.3 %reduce-scatter.14.cloned.1.call-start = ((), (), s32[]{:S(2)}) async-start(), calls=%async_computation.16 | async-start | bytes 5242880 | tf_op jit(solution)/shard_map/reduce_scatter | solution.py:495
  611.7 43.8 %collective-permute-start.49 = (bf16[2,64,2048]{2,1,0:T(8,128)(2,1)}, bf16[2,64,2048]{2,1,0:T(8,128)(2,1)}, u32[]{:S(2)}, u32[]{:S(2)}) collective-permute-start(bf16[2,64,2048]{2,1,0:T(8,128)(2,1)} %get-tuple-element.117), channel_id=1, source_target_pairs={{0,16},{1,17},{16,0},{17,1},{2,18},{3,19},{18,2},{19,3},{4,20},{5,... | collective-permute-start | bytes 1572872 | tf_op jit(solution)/shard_map/ppermute | solution.py:380
  613.0 34.8 %collective-permute-start.45 = (bf16[2,64,2048]{2,1,0:T(8,128)(2,1)}, bf16[2,64,2048]{2,1,0:T(8,128)(2,1)}, u32[]{:S(2)}, u32[]{:S(2)}) collective-permute-start(bf16[2,64,2048]{2,1,0:T(8,128)(2,1)} %get-tuple-element.119), channel_id=1, source_target_pairs={{0,16},{1,17},{16,0},{17,1},{2,18},{3,19},{18,2},{19,3},{4,20},{5,... | collective-permute-start | bytes 1572872 | tf_op jit(solution)/shard_map/ppermute | solution.py:380
  613.7 47.2 %collective-permute-start.44 = (bf16[2,64,2048]{2,1,0:T(8,128)(2,1)}, bf16[2,64,2048]{2,1,0:T(8,128)(2,1)}, u32[]{:S(2)}, u32[]{:S(2)}) collective-permute-start(bf16[2,64,2048]{2,1,0:T(8,128)(2,1)} %get-tuple-element.120), channel_id=1, source_target_pairs={{0,1},{1,0},{16,17},{17,16},{2,3},{3,2},{18,19},{19,18},{4,5},{5,4... | collective-permute-start | bytes 1572872 | tf_op jit(solution)/shard_map/ppermute | solution.py:380
  616.9 33.7 %collective-permute-start.47 = (bf16[2,64,2048]{2,1,0:T(8,128)(2,1)}, bf16[2,64,2048]{2,1,0:T(8,128)(2,1)}, u32[]{:S(2)}, u32[]{:S(2)}) collective-permute-start(bf16[2,64,2048]{2,1,0:T(8,128)(2,1)} %get-tuple-element.121), channel_id=1, source_target_pairs={{0,1},{1,0},{16,17},{17,16},{2,3},{3,2},{18,19},{19,18},{4,5},{5,4... | collective-permute-start | bytes 1572872 | tf_op jit(solution)/shard_map/ppermute | solution.py:380
  663.3 37.2 %collective-permute-start.55 = (bf16[2,64,2048]{2,1,0:T(8,128)(2,1)}, bf16[2,64,2048]{2,1,0:T(8,128)(2,1)}, u32[]{:S(2)}, u32[]{:S(2)}) collective-permute-start(bf16[2,64,2048]{2,1,0:T(8,128)(2,1)} %get-tuple-element.111), channel_id=1, source_target_pairs={{0,16},{1,17},{16,0},{17,1},{2,18},{3,19},{18,2},{19,3},{4,20},{5,... | collective-permute-start | bytes 1572872 | tf_op jit(solution)/shard_map/ppermute | solution.py:380
  666.7 33.8 %collective-permute-start.50 = (bf16[2,64,2048]{2,1,0:T(8,128)(2,1)S(1)}, bf16[2,64,2048]{2,1,0:T(8,128)(2,1)}, u32[]{:S(2)}, u32[]{:S(2)}) collective-permute-start(bf16[2,64,2048]{2,1,0:T(8,128)(2,1)S(1)} %get-tuple-element.114), channel_id=1, source_target_pairs={{0,1},{1,0},{16,17},{17,16},{2,3},{3,2},{18,19},{19,18},{4,5},{5,4... | collective-permute-start | bytes 1572872 | tf_op jit(solution)/shard_map/ppermute | solution.py:380
  672.9 76.9 %all-to-all-start.2 = ((bf16[4,64,2048]{2,1,0:T(8,128)(2,1)}), bf16[4,64,2048]{2,1,0:T(8,128)(2,1)S(1)}, u32[]{:S(2)}, u32[]{:S(2)}) async-start(bf16[4,64,2048]{2,1,0:T(8,128)(2,1)} %bitcast.370), calls=%async_computation.6 | async-start | bytes 2097152 | tf_op jit(solution)/shard_map/all_to_all | solution.py:428
  682.0 28.6 %collective-permute-start.54 = (bf16[2,64,2048]{2,1,0:T(8,128)(2,1)S(1)}, bf16[2,64,2048]{2,1,0:T(8,128)(2,1)S(1)}, u32[]{:S(2)}, u32[]{:S(2)}) collective-permute-start(bf16[2,64,2048]{2,1,0:T(8,128)(2,1)S(1)} %add_convert_fusion.8), channel_id=1, source_target_pairs={{0,16},{1,17},{16,0},{17,1},{2,18},{3,19},{18,2},{19,3},{4,20},{5,... | collective-permute-start | bytes 1572872 | tf_op jit(solution)/shard_map/ppermute | solution.py:380
  749.8 29.7 %all-to-all-start.3 = ((bf16[4,64,2048]{2,1,0:T(8,128)(2,1)}), bf16[4,64,2048]{2,1,0:T(8,128)(2,1)S(1)}, u32[]{:S(2)}, u32[]{:S(2)}) async-start(bf16[4,64,2048]{2,1,0:T(8,128)(2,1)} %bitcast.384), calls=%async_computation.7 | async-start | bytes 2097152 | tf_op jit(solution)/shard_map/all_to_all | solution.py:428
  (94 other events, 1209.5 us)
Sparse Core Ops, SparseCore 0:
  35.8 115.9 all-gather.3
  154.0 114.9 all-gather.5
  270.6 114.9 all-gather.7
  387.7 42.0 reduce-scatter.5
  432.1 76.0 reduce-scatter.7
  511.0 44.3 reduce-scatter.9
  557.7 76.0 reduce-scatter.11
  636.2 93.7 reduce-scatter.13

commit v3 on v2

--- a/solution.py
+++ b/solution.py
@@ -381,7 +381,7 @@
 
 
 def after(values, *others):
-    return lax.optimization_barrier((values,) + others)[0]
+    return lax.optimization_barrier((values,) + others)[0] if others else values
 
 
 def by_index(parts, index):
@@ -499,7 +499,11 @@
 
     def gain_settle(grads):
         def add(values, axis, size):
-            return sum((swap(values, axis, size, step) for step in range(1, size)), values)
+            step = 1
+            while step < size:
+                values = values + swap(values, axis, size, step)
+                step *= 2
+            return values
 
         grads = add(add(add(grads, group, nq), "core", 2), "ctx", nc)
         return pick(grads.reshape(2, 2 * nc * ny, rows), (core * nc + ctx) * ny + yi, 1)
@@ -524,10 +528,10 @@
 
         return jnp.concatenate(over_y(block), axis=0)
 
-    x_rows = rows_for(tokens)
+    held = prepare(wanted[0])
+    x_rows = rows_for(after(tokens, held))
+    weights = [fetch(held)]
     x_low = turn(x_rows)
-    held = prepare(wanted[0])
-    weights = [fetch(after(held, x_rows))]
     for sources in wanted[1:]:
         held = prepare(sources, held, x_rows)
         weights.append(fetch(held))
@@ -601,20 +605,23 @@
     one_terms = row_terms(back_one)
     mlp_terms = row_terms(after(mlp_out, residual_low), attn_held)
     block_out = turn(run_add_rows([after(residual, back_one)] + mlp_terms, outward))
+    received = jax.tree.leaves(one_terms)
+    one_terms[0] = after(one_terms[0], attn_summed)
     gain_one_grad, (inputs_grad,) = run_norm_backward(
         one_terms, x_low, gain_one, residual_grad, [BF16], SHORT, outward
     )
+    turned = turn(inputs_grad)
     block_out = pieces_out(after(block_out, inputs_grad))
-    grad_tokens = pieces_out(turn(inputs_grad)).astype(F32)
-    gain_grads = gain_settle(jnp.concatenate([gain_one_grad, gain_two_grad]))
-    mlp_grads = [
-        [
-            own_rows(after(summed, back_one if part + 1 < MLP_CHUNKS else inputs_grad), dim)
-            for summed, dim in pair
-        ]
-        for part, pair in enumerate(mlp_sums)
-    ]
+    gain_grads = gain_settle(
+        after(jnp.concatenate([gain_one_grad, gain_two_grad]), turned)
+    )
+    mlp_grads = []
+    for part, pair in enumerate(mlp_sums):
+        ready = [back_one] if part + 1 < MLP_CHUNKS else received
+        mlp_grads.append([own_rows(after(summed, *ready), dim) for summed, dim in pair])
+    grad_tokens = pieces_out(turned)
     attn_grads = own_rows(attn_summed, 0)
+    grad_tokens = after(grad_tokens, *attn_grads).astype(F32)
 
     grad_query, grad_key, grad_value = (
         jnp.concatenate(

time: 840 us -> 830 us (0.988)
    all_to_all x4, waiting for transfers between devices: 74.8 us -> 57 us  [turn(): return lax.all_to_all(pieces, 'ctx', 0, 0, tiled=True)]
    ppermute x74 -> x72, waiting for transfers between devices: 194 us -> 211 us  [swap(): return lax.ppermute(values, axis, [(i, i ^ step) for i in range(size)])]
    unnamed x115 -> x123, local copies, waits for them, and re-layouts: 26.8 us -> 17.2 us
    ppermute x74 -> x72, starting transfers between devices: 82.1 us -> 82.7 us  [swap(): return lax.ppermute(values, axis, [(i, i ^ step) for i in range(size)])]
  transfers between devices with their start and end apart: 86 -> 84, of which waited for: 40 -> 36; matrix products, arithmetic and copies ran while one was open for 33% -> 32% of each run, Pallas kernels for 16% -> 17%
where the time goes in v3:
time: 830 us; the launch traced here: 822 us
  waiting for transfers between devices  293 us (35%)
  matrix products  149 us (18%)
  Pallas kernels  136 us (16%)
  starting transfers between devices  101 us (12%)
  local copies, waits for them, and re-layouts  83.6 us (10%)
  other arithmetic  42.3 us (5%)
  between operations  16.3 us (2%)
    ppermute x72, waiting for transfers between devices, swap(): return lax.ppermute(values, axis, [(i, i ^ step) for i in range(size)])  211 us
    dot_general x19, matrix products, dot(): lax.dot_general(left, right, (contract, ((), ())), preferred_element_type...  149 us
    ppermute x72, starting transfers between devices, swap(): return lax.ppermute(values, axis, [(i, i ^ step) for i in range(size)])  82.7 us
    all_to_all x4, waiting for transfers between devices, turn(): return lax.all_to_all(pieces, 'ctx', 0, 0, tiled=True)  57 us
    pallas_call x2, Pallas kernels, run_feed_forward(): pl.pallas_call(feed_forward, grid=(part_cols // tile,), in_specs=[whole,...  39.7 us
    pallas_call x1, Pallas kernels, run_attention_backward(): pl.pallas_call(attention_backward, grid=(pairs, 3), in_specs=[column(0),...  36.3 us
    dynamic_update_slice x20, local copies, waits for them, and re-layouts, put(): lax.dynamic_update_slice(out, part[:, None], (start, quarter ^ step, 0, 0))  20.9 us
    pallas_call x1, Pallas kernels, run_attention_forward(): pl.pallas_call(attention_forward, grid=(pairs,), in_specs=[column(0), col...  19.8 us
  transfers between devices with their start and end apart: 84, of which 36 were waited for; matrix products, arithmetic and copies ran while one was open for 32% of the time, Pallas kernels for 17%

profile of v3, /device:TPU:0, one launch (start us, length us, event | category | flops | bytes accessed | tf_op | source)
XLA Modules:
  0.0 821.8 jit_solution(9292835442105488914)
XLA Ops:
  13.8 11.8 %collective-permute-done = bf16[128,2048]{1,0:T(8,128)(2,1)S(1)} collective-permute-done((bf16[128,2048]{1,0:T(8,128)(2,1)S(1)}, bf16[128,2048]{1,0:T(8,128)(2,1)S(1)}, u32[]{:S(2)}, u32[]{:S(2)}) %collective-permute-start) | collective-permute-done | bytes 524320 | tf_op jit(solution)/shard_map/ppermute | solution.py:380
  66.1 11.1 %collective-permute-done.1 = bf16[2,64,2048]{2,1,0:T(8,128)(2,1)S(1)} collective-permute-done((bf16[2,64,2048]{2,1,0:T(8,128)(2,1)S(1)}, bf16[2,64,2048]{2,1,0:T(8,128)(2,1)S(1)}, u32[]{:S(2)}, u32[]{:S(2)}) %collective-permute-start.1) | collective-permute-done | bytes 524320 | tf_op jit(solution)/shard_map/ppermute | solution.py:380
  81.0 34.1 %all-to-all-done.1 = bf16[4,64,2048]{2,1,0:T(8,128)(2,1)S(1)} async-done(((bf16[4,64,2048]{2,1,0:T(8,128)(2,1)}), bf16[4,64,2048]{2,1,0:T(8,128)(2,1)S(1)}, u32[]{:S(2)}, u32[]{:S(2)}) %all-to-all-start.1) | async-done | bytes 1048608 | tf_op jit(solution)/shard_map/all_to_all | solution.py:428
  130.9 22.9 %all-to-all-done = bf16[4,64,2048]{2,1,0:T(8,128)(2,1)S(1)} async-done(((bf16[4,64,2048]{2,1,0:T(8,128)(2,1)}), bf16[4,64,2048]{2,1,0:T(8,128)(2,1)S(1)}, u32[]{:S(2)}, u32[]{:S(2)}) %all-to-all-start) | async-done | bytes 1048608 | tf_op jit(solution)/shard_map/all_to_all | solution.py:428
  167.9 15.9 %collective-permute-done.7 = bf16[4,64,2048]{2,1,0:T(8,128)(2,1)S(1)} collective-permute-done((bf16[4,64,2048]{2,1,0:T(8,128)(2,1)}, bf16[4,64,2048]{2,1,0:T(8,128)(2,1)S(1)}, u32[]{:S(2)}, u32[]{:S(2)}) %collective-permute-start.7) | collective-permute-done | bytes 1048608 | tf_op jit(solution)/shard_map/ppermute | solution.py:380
  189.0 7.9 collective-permute-done.8
  201.5 12.0 %fusion.4.q_ref.k_ref.v_ref = f32[1024,1536]{1,0:T(8,128)} fusion(bf16[1024,2048]{1,0:T(8,128)(2,1)} %bitcast.17, bf16[2048,2048]{1,0:T(8,128)(2,1)} %all-gather.4.cloned.1.call-done.right_ref), kind=kOutput, calls=%fused_computation.8 | convolution fusion | flops 6442450944 | bytes 16777216 | tf_op jit(solution)/shard_map/dot_general | solution.py:48
  214.5 19.8 %attention_forward.1 = (bf16[1024,512]{1,0:T(8,128)(2,1)}, f32[1024,512]{1,0:T(8,128)}) custom-call(f32[1024,1536]{1,0:T(8,128)} %fusion.4.q_ref.k_ref.v_ref, f32[1024,1536]{1,0:T(8,128)} %fusion.4.q_ref.k_ref.v_ref, f32[1024,1536]{1,0:T(8,128)} %fusion.4.q_ref.k_ref.v_ref, f32[1024,128]{1,0:T(8,128)} %get-tuple-element.264.cos_ref, ...), custom_call_target="tpu_custom_call" | custom-call | flops 999999995904 | bytes 1000000 | tf_op jit(solution)/shard_map/attention_forward/pallas_call | solution.py:152
  269.1 7.5 collective-permute-done.11
  299.8 12.2 %collective-permute-done.18 = bf16[4,64,2048]{2,1,0:T(8,128)(2,1)S(1)} collective-permute-done((bf16[4,64,2048]{2,1,0:T(8,128)(2,1)}, bf16[4,64,2048]{2,1,0:T(8,128)(2,1)S(1)}, u32[]{:S(2)}, u32[]{:S(2)}) %collective-permute-start.18) | collective-permute-done | bytes 1048608 | tf_op jit(solution)/shard_map/ppermute | solution.py:380
  326.2 20.1 %feed_forward.2 = (bf16[1024,1024]{1,0:T(8,128)(2,1)}, bf16[1024,2048]{1,0:T(8,128)(2,1)}) custom-call(bf16[1024,2048]{1,0:T(8,128)(2,1)} %bitcast.47.normed_ref, bf16[1024,2048]{1,0:T(8,128)(2,1)} %bitcast.62.above_ref, bf16[2048,3072]{1,0:T(8,128)(2,1)} %all-gather.6.cloned.1.call-done.gate_up_ref.down_ref, ...), custom_call_target="tpu_custom_call" | custom-call | flops 999999995904 | bytes 1000000 | tf_op jit(solution)/shard_map/feed_forward/pallas_call | solution.py:356
  352.4 7.9 convolution_convert_fusion.3
  368.0 10.8 %add_convert_fusion.3 = bf16[1024,2048]{1,0:T(8,128)(2,1)} fusion(bf16[1024,2048]{1,0:T(8,128)(2,1)} %collective-permute-done.27, bf16[1024,2048]{1,0:T(8,128)(2,1)} %get-tuple-element.61, bf16[1024,2048]{1,0:T(8,128)(2,1)} %bitcast.47.normed_ref, s32[]{:T(128)S(6)} %select_n.504), kind=kOutput, calls=%fused_computation.7 | convolution fusion | flops 4301258752 | bytes 14680068 | tf_op jit(solution)/shard_map/dot_general | solution.py:48
  385.9 19.6 %feed_forward.3 = (bf16[1024,1024]{1,0:T(8,128)(2,1)}, bf16[1024,2048]{1,0:T(8,128)(2,1)}) custom-call(bf16[1024,2048]{1,0:T(8,128)(2,1)} %bitcast.47.normed_ref, bf16[1024,2048]{1,0:T(8,128)(2,1)} %bitcast.62.above_ref, bf16[2048,3072]{1,0:T(8,128)(2,1)} %all-gather.8.cloned.1.call-done.gate_up_ref.down_ref, ...), custom_call_target="tpu_custom_call" | custom-call | flops 999999995904 | bytes 1000000 | tf_op jit(solution)/shard_map/feed_forward/pallas_call | solution.py:356
  405.5 14.8 %fusion = f32[1024,2048]{1,0:T(8,128)} fusion(bf16[1024,2048]{1,0:T(8,128)(2,1)} %get-tuple-element.68, bf16[2048,3072]{1,0:T(8,128)(2,1)} %all-gather.8.cloned.1.call-done.gate_up_ref.down_ref), kind=kOutput, calls=%fused_computation | convolution fusion | flops 8589934592 | bytes 20971520 | tf_op jit(solution)/shard_map/dot_general | solution.py:48
  420.3 12.5 %add_convert_fusion.2 = bf16[1024,2048]{1,0:T(8,128)(2,1)S(1)} fusion(f32[1024,2048]{1,0:T(8,128)} %fusion, bf16[1024,2048]{1,0:T(8,128)(2,1)} %get-tuple-element.61, bf16[2048,3072]{1,0:T(8,128)(2,1)S(1)} %copy-done.28), kind=kOutput, calls=%fused_computation.6 | convolution fusion | flops 8594128896 | bytes 25165824 | tf_op jit(solution)/shard_map/dot_general | solution.py:48
  432.8 10.9 %convolution_convert_fusion.2 = bf16[1024,2048]{1,0:T(8,128)(2,1)} fusion(bf16[1024,2048]{1,0:T(8,128)(2,1)} %get-tuple-element.68, bf16[1024,2048]{1,0:T(8,128)(2,1)} %bitcast.47.normed_ref, s32[]{:T(128)S(6)} %select_n.505), kind=kOutput, calls=%fused_computation.20 | convolution fusion | flops 4297064448 | bytes 10485764 | tf_op jit(solution)/shard_map/dot_general | solution.py:48
  452.1 9.2 %fusion.8 = f32[1024,2048]{1,0:T(8,128)} fusion(bf16[1024,1024]{1,0:T(8,128)(2,1)S(1)} %copy-done.42, bf16[2048,3072]{1,0:T(8,128)(2,1)} %all-gather.8.cloned.1.call-done.gate_up_ref.down_ref), kind=kOutput, calls=%fused_computation.11 | convolution fusion | flops 4294967296 | bytes 14680064 | tf_op jit(solution)/shard_map/dot_general | solution.py:48
  461.3 9.7 %add_convert_fusion = bf16[1024,2048]{1,0:T(8,128)(2,1)} fusion(f32[1024,2048]{1,0:T(8,128)} %fusion.8, bf16[1024,1024]{1,0:T(8,128)(2,1)S(1)} %copy-done.41, bf16[2048,3072]{1,0:T(8,128)(2,1)} %all-gather.6.cloned.1.call-done.gate_up_ref.down_ref), kind=kOutput, calls=%fused_computation.4 | convolution fusion | flops 4299161600 | bytes 18874368 | tf_op jit(solution)/shard_map/dot_general | solution.py:48
  477.2 10.7 %add_convert_fusion.1 = bf16[1024,2048]{1,0:T(8,128)(2,1)} fusion(bf16[1024,2048]{1,0:T(8,128)(2,1)} %collective-permute-done.31, bf16[1024,2048]{1,0:T(8,128)(2,1)} %get-tuple-element.68, bf16[1024,2048]{1,0:T(8,128)(2,1)} %bitcast.47.normed_ref, s32[]{:T(128)S(6)} %select_n.504), kind=kOutput, calls=%fused_computation.5 | convolution fusion | flops 4301258752 | bytes 14680068 | tf_op jit(solution)/shard_map/dot_general | solution.py:48
  495.7 12.9 %reduce-scatter.8.cloned.1.call-done = bf16[256,2048]{1,0:T(8,128)(2,1)} async-done(((bf16[1024,2048]{1,0:T(8,128)(2,1)}), bf16[256,2048]{1,0:T(8,128)(2,1)}) %reduce-scatter.8.cloned.1.call-update) | async-done | bytes 1048592 | tf_op jit(solution)/shard_map/reduce_scatter | solution.py:495
  519.0 21.5 %collective-permute-done.39 = bf16[4,64,2048]{2,1,0:T(8,128)(2,1)S(1)} collective-permute-done((bf16[4,64,2048]{2,1,0:T(8,128)(2,1)}, bf16[4,64,2048]{2,1,0:T(8,128)(2,1)S(1)}, u32[]{:S(2)}, u32[]{:S(2)}) %collective-permute-start.39) | collective-permute-done | bytes 1048608 | tf_op jit(solution)/shard_map/ppermute | solution.py:380
  543.9 9.6 %collective-permute-done.40 = bf16[2,64,2048]{2,1,0:T(8,128)(2,1)S(1)} collective-permute-done((bf16[2,64,2048]{2,1,0:T(8,128)(2,1)S(1)}, bf16[2,64,2048]{2,1,0:T(8,128)(2,1)S(1)}, u32[]{:S(2)}, u32[]{:S(2)}) %collective-permute-start.40) | collective-permute-done | bytes 524320 | tf_op jit(solution)/shard_map/ppermute | solution.py:380
  561.3 36.3 %attention_backward.1.left_ref = bf16[1024,1536]{1,0:T(8,128)(2,1)} custom-call(f32[1024,1536]{1,0:T(8,128)} %fusion.4.q_ref.k_ref.v_ref, f32[1024,1536]{1,0:T(8,128)} %fusion.4.q_ref.k_ref.v_ref, f32[1024,1536]{1,0:T(8,128)} %fusion.4.q_ref.k_ref.v_ref, bf16[1024,512]{1,0:T(8,128)(2,1)} %fusion.34.do_ref, f32[1024,512]{1,0:T(8,128)} %get-tuple-element.74.lse_ref, ...), custom_call_target="tpu_custom_call" | custom-call | flops 10000000000 | bytes 1000000 | tf_op jit(solution)/shard_map/attention_backward/pallas_call | solution.py:172
  597.6 7.8 convolution_convert_fusion.1
  634.2 12.3 %turned_product.1 = bf16[1024,2048]{1,0:T(8,128)(2,1)} custom-call(bf16[1024,1536]{1,0:T(8,128)(2,1)} %attention_backward.1.left_ref, bf16[2048,2048]{1,0:T(8,128)(2,1)} %all-gather.4.cloned.1.call-done.right_ref), custom_call_target="tpu_custom_call" | custom-call | flops 999999995904 | bytes 1000000 | tf_op jit(solution)/shard_map/turned_product/pallas_call | solution.py:337
  690.9 9.9 %collective-permute-done.55 = bf16[2,64,2048]{2,1,0:T(8,128)(2,1)} collective-permute-done((bf16[2,64,2048]{2,1,0:T(8,128)(2,1)}, bf16[2,64,2048]{2,1,0:T(8,128)(2,1)}, u32[]{:S(2)}, u32[]{:S(2)}) %collective-permute-start.55) | collective-permute-done | bytes 524320 | tf_op jit(solution)/shard_map/ppermute | solution.py:380
  700.8 10.2 %collective-permute-done.54 = bf16[2,64,2048]{2,1,0:T(8,128)(2,1)S(1)} collective-permute-done((bf16[2,64,2048]{2,1,0:T(8,128)(2,1)S(1)}, bf16[2,64,2048]{2,1,0:T(8,128)(2,1)S(1)}, u32[]{:S(2)}, u32[]{:S(2)}) %collective-permute-start.54) | collective-permute-done | bytes 524320 | tf_op jit(solution)/shard_map/ppermute | solution.py:380
  722.7 7.9 collective-permute-done.69
  753.9 9.3 %collective-permute-done.58 = bf16[2,64,2048]{2,1,0:T(8,128)(2,1)S(1)} collective-permute-done((bf16[2,64,2048]{2,1,0:T(8,128)(2,1)S(1)}, bf16[2,64,2048]{2,1,0:T(8,128)(2,1)S(1)}, u32[]{:S(2)}, u32[]{:S(2)}) %collective-permute-start.58) | collective-permute-done | bytes 524320 | tf_op jit(solution)/shard_map/ppermute | solution.py:380
  763.1 10.7 %collective-permute-done.57 = bf16[2,64,2048]{2,1,0:T(8,128)(2,1)S(1)} collective-permute-done((bf16[2,64,2048]{2,1,0:T(8,128)(2,1)S(1)}, bf16[2,64,2048]{2,1,0:T(8,128)(2,1)S(1)}, u32[]{:S(2)}, u32[]{:S(2)}) %collective-permute-start.57) | collective-permute-done | bytes 524320 | tf_op jit(solution)/shard_map/ppermute | solution.py:380
  800.0 10.4 %collective-permute-done.60 = bf16[2,64,2048]{2,1,0:T(8,128)(2,1)S(1)} collective-permute-done((bf16[2,64,2048]{2,1,0:T(8,128)(2,1)}, bf16[2,64,2048]{2,1,0:T(8,128)(2,1)S(1)}, u32[]{:S(2)}, u32[]{:S(2)}) %collective-permute-start.60) | collective-permute-done | bytes 524320 | tf_op jit(solution)/shard_map/ppermute | solution.py:380
  (421 shorter events, 364.9 us)
Async XLA Ops:
  7.2 194.3 %all-gather.4.cloned.1.call-start = ((), (), s32[]{:S(2)}) async-start(), calls=%async_computation.9 | async-start | bytes 9437184 | tf_op jit(solution)/shard_map/all_gather | solution.py:477
  28.8 36.0 %collective-permute-start.10 = (s32[2,1024]{1,0:T(2,128)S(1)}, s32[2,1024]{1,0:T(2,128)S(1)}, u32[]{:S(2)}, u32[]{:S(2)}) collective-permute-start(s32[2,1024]{1,0:T(2,128)S(1)} %copy-done.24), channel_id=1, source_target_pairs={{0,16},{16,0},{1,17},{17,1},{2,18},{18,2},{3,19},{19,3},{4,20},{20... | collective-permute-start | bytes 24584 | tf_op jit(solution)/shard_map/ppermute | solution.py:380
  58.1 57.0 %all-to-all-start.1 = ((bf16[4,64,2048]{2,1,0:T(8,128)(2,1)}), bf16[4,64,2048]{2,1,0:T(8,128)(2,1)S(1)}, u32[]{:S(2)}, u32[]{:S(2)}) async-start(bf16[4,64,2048]{2,1,0:T(8,128)(2,1)} %pad_maximum_fusion.7), calls=%async_computation.1 | async-start | bytes 2097152 | tf_op jit(solution)/shard_map/all_to_all | solution.py:428
  79.4 43.9 %collective-permute-start.26 = (bf16[128,3072]{1,0:T(8,128)(2,1)}, bf16[128,3072]{1,0:T(8,128)(2,1)}, u32[]{:S(2)}, u32[]{:S(2)}) collective-permute-start(bf16[128,3072]{1,0:T(8,128)(2,1)} %bitcast_dynamic-update-slice_fusion.20), channel_id=1, source_target_pairs={{0,16},{16,0},{1,17},{17,1},{2,18},{18,2},{3,19},{19,3},{4,20},{20... | collective-permute-start | bytes 2359304 | tf_op jit(solution)/shard_map/ppermute | solution.py:380
  115.1 38.7 %all-to-all-start = ((bf16[4,64,2048]{2,1,0:T(8,128)(2,1)}), bf16[4,64,2048]{2,1,0:T(8,128)(2,1)S(1)}, u32[]{:S(2)}, u32[]{:S(2)}) async-start(bf16[4,64,2048]{2,1,0:T(8,128)(2,1)} %pad_maximum_fusion.6), calls=%async_computation | async-start | bytes 2097152 | tf_op jit(solution)/shard_map/all_to_all | solution.py:428
  119.5 206.7 %all-gather.6.cloned.1.call-start = ((), (), s32[]{:S(2)}) async-start(), calls=%async_computation.10 | async-start | bytes 14155776 | tf_op jit(solution)/shard_map/all_gather | solution.py:477
  125.8 260.2 %all-gather.8.cloned.1.call-start = ((), (), s32[]{:S(2)}) async-start(), calls=%async_computation.11 | async-start | bytes 14155776 | tf_op jit(solution)/shard_map/all_gather | solution.py:477
  125.8 35.7 %collective-permute-start.29 = (bf16[128,3072]{1,0:T(8,128)(2,1)}, bf16[128,3072]{1,0:T(8,128)(2,1)}, u32[]{:S(2)}, u32[]{:S(2)}) collective-permute-start(bf16[128,3072]{1,0:T(8,128)(2,1)} %copy-done.27), channel_id=1, source_target_pairs={{0,16},{16,0},{1,17},{17,1},{2,18},{18,2},{3,19},{19,3},{4,20},{20... | collective-permute-start | bytes 2359304 | tf_op jit(solution)/shard_map/ppermute | solution.py:380
  164.2 331.4 %reduce-scatter.6.cloned.1.call-start = ((), (), s32[]{:S(2)}) async-start(), calls=%async_computation.12 | async-start | bytes 2621440 | tf_op jit(solution)/shard_map/reduce_scatter | solution.py:495
  199.0 46.5 %collective-permute-start.23 = (bf16[4,64,2048]{2,1,0:T(8,128)(2,1)}, bf16[4,64,2048]{2,1,0:T(8,128)(2,1)}, u32[]{:S(2)}, u32[]{:S(2)}) collective-permute-start(bf16[4,64,2048]{2,1,0:T(8,128)(2,1)} %bitcast.52), channel_id=1, source_target_pairs={{0,16},{1,17},{16,0},{17,1},{2,18},{3,19},{18,2},{19,3},{4,20},{5,... | collective-permute-start | bytes 3145736 | tf_op jit(solution)/shard_map/ppermute | solution.py:380
  200.5 48.1 %collective-permute-start.22 = (bf16[4,64,2048]{2,1,0:T(8,128)(2,1)}, bf16[4,64,2048]{2,1,0:T(8,128)(2,1)}, u32[]{:S(2)}, u32[]{:S(2)}) collective-permute-start(bf16[4,64,2048]{2,1,0:T(8,128)(2,1)} %bitcast.52), channel_id=1, source_target_pairs={{0,1},{1,0},{16,17},{17,16},{2,3},{3,2},{18,19},{19,18},{4,5},{5,4... | collective-permute-start | bytes 3145736 | tf_op jit(solution)/shard_map/ppermute | solution.py:380
  247.4 45.0 %collective-permute-start.24 = (bf16[2,64,2048]{2,1,0:T(8,128)(2,1)}, bf16[2,64,2048]{2,1,0:T(8,128)(2,1)}, u32[]{:S(2)}, u32[]{:S(2)}) collective-permute-start(bf16[2,64,2048]{2,1,0:T(8,128)(2,1)} %slice.447), channel_id=1, source_target_pairs={{0,1},{1,0},{16,17},{17,16},{2,3},{3,2},{18,19},{19,18},{4,5},{5,4... | collective-permute-start | bytes 1572872 | tf_op jit(solution)/shard_map/ppermute | solution.py:380
  256.4 28.0 %collective-permute-start.13 = (bf16[2,64,2048]{2,1,0:T(8,128)(2,1)S(1)}, bf16[2,64,2048]{2,1,0:T(8,128)(2,1)S(1)}, u32[]{:S(2)}, u32[]{:S(2)}) collective-permute-start(bf16[2,64,2048]{2,1,0:T(8,128)(2,1)S(1)} %get-tuple-element.140), channel_id=1, source_target_pairs={{0,1},{1,0},{16,17},{17,16},{2,3},{3,2},{18,19},{19,18},{4,5},{5,4... | collective-permute-start | bytes 1572872 | tf_op jit(solution)/shard_map/ppermute | solution.py:380
  366.8 141.8 %reduce-scatter.8.cloned.1.call-start = ((), (), s32[]{:S(2)}) async-start(), calls=%async_computation.13 | async-start | bytes 5242880 | tf_op jit(solution)/shard_map/reduce_scatter | solution.py:495
  378.9 250.1 %reduce-scatter.10.cloned.1.call-start = ((), (), s32[]{:S(2)}) async-start(), calls=%async_computation.14 | async-start | bytes 2621440 | tf_op jit(solution)/shard_map/reduce_scatter | solution.py:495
  443.8 33.4 %collective-permute-start.31 = (bf16[1024,2048]{1,0:T(8,128)(2,1)}, bf16[1024,2048]{1,0:T(8,128)(2,1)}, u32[]{:S(2)}, u32[]{:S(2)}) collective-permute-start(bf16[1024,2048]{1,0:T(8,128)(2,1)} %convolution_convert_fusion.2), channel_id=1, source_target_pairs={{0,8},{8,0},{1,9},{9,1},{2,10},{10,2},{3,11},{11,3},{4,12},{12,4},... | collective-permute-start | bytes 12582920 | tf_op jit(solution)/shard_map/ppermute | solution.py:380
  444.4 64.2 %collective-permute-start.37 = (bf16[2,64,2048]{2,1,0:T(8,128)(2,1)S(1)}, bf16[2,64,2048]{2,1,0:T(8,128)(2,1)}, u32[]{:S(2)}, u32[]{:S(2)}) collective-permute-start(bf16[2,64,2048]{2,1,0:T(8,128)(2,1)S(1)} %get-tuple-element.129), channel_id=1, source_target_pairs={{0,16},{1,17},{16,0},{17,1},{2,18},{3,19},{18,2},{19,3},{4,20},{5,... | collective-permute-start | bytes 1572872 | tf_op jit(solution)/shard_map/ppermute | solution.py:380
  445.9 42.0 %collective-permute-start.33 = (bf16[2,64,2048]{2,1,0:T(8,128)(2,1)S(1)}, bf16[2,64,2048]{2,1,0:T(8,128)(2,1)}, u32[]{:S(2)}, u32[]{:S(2)}) collective-permute-start(bf16[2,64,2048]{2,1,0:T(8,128)(2,1)S(1)} %get-tuple-element.131), channel_id=1, source_target_pairs={{0,16},{1,17},{16,0},{17,1},{2,18},{3,19},{18,2},{19,3},{4,20},{5,... | collective-permute-start | bytes 1572872 | tf_op jit(solution)/shard_map/ppermute | solution.py:380
  446.5 62.1 %collective-permute-start.30 = (bf16[2,64,2048]{2,1,0:T(8,128)(2,1)S(1)}, bf16[2,64,2048]{2,1,0:T(8,128)(2,1)}, u32[]{:S(2)}, u32[]{:S(2)}) collective-permute-start(bf16[2,64,2048]{2,1,0:T(8,128)(2,1)S(1)} %get-tuple-element.132), channel_id=1, source_target_pairs={{0,1},{1,0},{16,17},{17,16},{2,3},{3,2},{18,19},{19,18},{4,5},{5,4... | collective-permute-start | bytes 1572872 | tf_op jit(solution)/shard_map/ppermute | solution.py:380
  495.6 138.6 %reduce-scatter.12.cloned.1.call-start = ((), (), s32[]{:S(2)}) async-start(), calls=%async_computation.15 | async-start | bytes 5242880 | tf_op jit(solution)/shard_map/reduce_scatter | solution.py:495
  518.3 215.8 %reduce-scatter.14.cloned.1.call-start = ((), (), s32[]{:S(2)}) async-start(), calls=%async_computation.16 | async-start | bytes 5242880 | tf_op jit(solution)/shard_map/reduce_scatter | solution.py:495
  612.0 43.6 %collective-permute-start.49 = (bf16[2,64,2048]{2,1,0:T(8,128)(2,1)}, bf16[2,64,2048]{2,1,0:T(8,128)(2,1)}, u32[]{:S(2)}, u32[]{:S(2)}) collective-permute-start(bf16[2,64,2048]{2,1,0:T(8,128)(2,1)} %get-tuple-element.123), channel_id=1, source_target_pairs={{0,16},{1,17},{16,0},{17,1},{2,18},{3,19},{18,2},{19,3},{4,20},{5,... | collective-permute-start | bytes 1572872 | tf_op jit(solution)/shard_map/ppermute | solution.py:380
  613.3 34.9 %collective-permute-start.45 = (bf16[2,64,2048]{2,1,0:T(8,128)(2,1)}, bf16[2,64,2048]{2,1,0:T(8,128)(2,1)}, u32[]{:S(2)}, u32[]{:S(2)}) collective-permute-start(bf16[2,64,2048]{2,1,0:T(8,128)(2,1)} %get-tuple-element.125), channel_id=1, source_target_pairs={{0,16},{1,17},{16,0},{17,1},{2,18},{3,19},{18,2},{19,3},{4,20},{5,... | collective-permute-start | bytes 1572872 | tf_op jit(solution)/shard_map/ppermute | solution.py:380
  614.0 43.1 %collective-permute-start.44 = (bf16[2,64,2048]{2,1,0:T(8,128)(2,1)}, bf16[2,64,2048]{2,1,0:T(8,128)(2,1)}, u32[]{:S(2)}, u32[]{:S(2)}) collective-permute-start(bf16[2,64,2048]{2,1,0:T(8,128)(2,1)} %get-tuple-element.126), channel_id=1, source_target_pairs={{0,1},{1,0},{16,17},{17,16},{2,3},{3,2},{18,19},{19,18},{4,5},{5,4... | collective-permute-start | bytes 1572872 | tf_op jit(solution)/shard_map/ppermute | solution.py:380
  617.2 33.7 %collective-permute-start.47 = (bf16[2,64,2048]{2,1,0:T(8,128)(2,1)}, bf16[2,64,2048]{2,1,0:T(8,128)(2,1)}, u32[]{:S(2)}, u32[]{:S(2)}) collective-permute-start(bf16[2,64,2048]{2,1,0:T(8,128)(2,1)} %get-tuple-element.127), channel_id=1, source_target_pairs={{0,1},{1,0},{16,17},{17,16},{2,3},{3,2},{18,19},{19,18},{4,5},{5,4... | collective-permute-start | bytes 1572872 | tf_op jit(solution)/shard_map/ppermute | solution.py:380
  660.8 28.7 %collective-permute-start.68 = (bf16[128,2048]{1,0:T(8,128)(2,1)}, bf16[128,2048]{1,0:T(8,128)(2,1)}, u32[]{:S(2)}, u32[]{:S(2)}) collective-permute-start(bf16[128,2048]{1,0:T(8,128)(2,1)} %constant_dynamic-slice_fusion.5), channel_id=1, source_target_pairs={{0,16},{16,0},{1,17},{17,1},{2,18},{18,2},{3,19},{19,3},{4,20},{20... | collective-permute-start | bytes 1572872 | tf_op jit(solution)/shard_map/ppermute | solution.py:380
  664.3 36.5 %collective-permute-start.55 = (bf16[2,64,2048]{2,1,0:T(8,128)(2,1)}, bf16[2,64,2048]{2,1,0:T(8,128)(2,1)}, u32[]{:S(2)}, u32[]{:S(2)}) collective-permute-start(bf16[2,64,2048]{2,1,0:T(8,128)(2,1)} %get-tuple-element.117), channel_id=1, source_target_pairs={{0,16},{1,17},{16,0},{17,1},{2,18},{3,19},{18,2},{19,3},{4,20},{5,... | collective-permute-start | bytes 1572872 | tf_op jit(solution)/shard_map/ppermute | solution.py:380
  667.0 33.8 %collective-permute-start.50 = (bf16[2,64,2048]{2,1,0:T(8,128)(2,1)}, bf16[2,64,2048]{2,1,0:T(8,128)(2,1)}, u32[]{:S(2)}, u32[]{:S(2)}) collective-permute-start(bf16[2,64,2048]{2,1,0:T(8,128)(2,1)} %get-tuple-element.119), channel_id=1, source_target_pairs={{0,1},{1,0},{16,17},{17,16},{2,3},{3,2},{18,19},{19,18},{4,5},{5,4... | collective-permute-start | bytes 1572872 | tf_op jit(solution)/shard_map/ppermute | solution.py:380
  673.3 69.7 %all-to-all-start.2 = ((bf16[4,64,2048]{2,1,0:T(8,128)(2,1)}), bf16[4,64,2048]{2,1,0:T(8,128)(2,1)S(1)}, u32[]{:S(2)}, u32[]{:S(2)}) async-start(bf16[4,64,2048]{2,1,0:T(8,128)(2,1)} %bitcast.384), calls=%async_computation.6 | async-start | bytes 2097152 | tf_op jit(solution)/shard_map/all_to_all | solution.py:428
  680.3 30.7 %collective-permute-start.54 = (bf16[2,64,2048]{2,1,0:T(8,128)(2,1)S(1)}, bf16[2,64,2048]{2,1,0:T(8,128)(2,1)S(1)}, u32[]{:S(2)}, u32[]{:S(2)}) collective-permute-start(bf16[2,64,2048]{2,1,0:T(8,128)(2,1)S(1)} %get-tuple-element.121), channel_id=1, source_target_pairs={{0,16},{1,17},{16,0},{17,1},{2,18},{3,19},{18,2},{19,3},{4,20},{5,... | collective-permute-start | bytes 1572872 | tf_op jit(solution)/shard_map/ppermute | solution.py:380
  681.9 29.0 %collective-permute-start.52 = (bf16[2,64,2048]{2,1,0:T(8,128)(2,1)S(1)}, bf16[2,64,2048]{2,1,0:T(8,128)(2,1)S(1)}, u32[]{:S(2)}, u32[]{:S(2)}) collective-permute-start(bf16[2,64,2048]{2,1,0:T(8,128)(2,1)S(1)} %get-tuple-element.122), channel_id=1, source_target_pairs={{0,1},{1,0},{16,17},{17,16},{2,3},{3,2},{18,19},{19,18},{4,5},{5,4... | collective-permute-start | bytes 1572872 | tf_op jit(solution)/shard_map/ppermute | solution.py:380
  743.0 32.7 %all-to-all-start.3 = ((bf16[4,64,2048]{2,1,0:T(8,128)(2,1)}), bf16[4,64,2048]{2,1,0:T(8,128)(2,1)S(1)}, u32[]{:S(2)}, u32[]{:S(2)}) async-start(bf16[4,64,2048]{2,1,0:T(8,128)(2,1)} %bitcast.398), calls=%async_computation.8 | async-start | bytes 2097152 | tf_op jit(solution)/shard_map/all_to_all | solution.py:428
  (96 other events, 1374.9 us)
Sparse Core Ops, SparseCore 0:
  27.1 125.1 all-gather.3
  154.4 114.8 all-gather.5
  270.9 114.9 all-gather.7
  388.1 42.0 reduce-scatter.5
  432.4 76.0 reduce-scatter.7
  511.3 44.3 reduce-scatter.9
  558.1 76.0 reduce-scatter.11
  636.5 93.7 reduce-scatter.13
